TPU v7x, 256 devices: a whole 4x4x8 slice. The times are simulated.
256 devices in a mesh: freq: 4 (over x), rx: 16 (over z, core), src: 4 (over y).
Axes of the slice: x: 4, y: 4, z: 8, core: 2. Of those that a mesh axis runs over, the one named last changes fastest.
Arguments:
- kernel: bfloat16 [2, 4, 8192, 8192], P(None, 'freq', 'rx', 'src'), may hold values from -5 to 5
- data: float32 [2, 4, 8192, 128], P(None, 'freq', 'rx'), may hold values from -100 to 100
Outputs:
- solution: float32 [2, 4, 8192, 128], P(None, 'freq', 'src')
- direction: float32 [2, 4, 8192, 128], P(None, 'freq', 'src')
All inputs are finite; a program needn't handle non-finite values.
Results may differ from a plain program's by a relative error of at most 0.011.
Values may be sent and summed in bfloat16 or wider, within the bound.
A program may use at most 64 MiB of HBM per device.

v0:
```python
import math

import jax
import jax.numpy as jnp
from jax import lax
from jax.sharding import PartitionSpec as P

ITERS = 2


def on_device(kernel, data):
    real_part = kernel[0, 0]
    imag_part = kernel[1, 0]
    width = data.shape[3]
    cols_local = real_part.shape[1]
    dims = (((0,), (0,)), ((), ()))
    start_cat = jnp.concatenate([data[0, 0], data[1, 0]], axis=1)

    def adjoint_term(piece):
        swapped = jnp.concatenate([piece[:, width:], -piece[:, :width]], axis=1)
        term = lax.dot_general(real_part, piece, dims, preferred_element_type=jnp.float32)
        return term + lax.dot_general(imag_part, swapped, dims, preferred_element_type=jnp.float32)

    def adjoint(u_state):
        rounded = u_state.astype(jnp.bfloat16)
        partial_sum = adjoint_term(rounded)
        return lax.psum(partial_sum, "rx")

    def data_norm(field):
        local = jnp.sum(field * field)
        total = lax.psum(local, ("freq", "rx"))
        return jnp.sqrt(total)

    def model_norm(field):
        local = jnp.sum(field * field)
        total = lax.psum(local, ("freq", "src"))
        return jnp.sqrt(total)

    u_state = start_cat
    beta = data_norm(u_state)
    u_state = u_state / beta
    q_state = adjoint(u_state)
    alpha = model_norm(q_state)
    v_state = q_state / alpha
    w_state = v_state
    x_state = jnp.zeros_like(v_state)
    phibar = beta
    rhobar = alpha
    for step in range(ITERS):
        forward_rounded = v_state.astype(jnp.bfloat16)
        first = jnp.dot(real_part, forward_rounded, preferred_element_type=jnp.float32)
        second = jnp.dot(imag_part, forward_rounded, preferred_element_type=jnp.float32)
        forward_partial_sum = jnp.concatenate(
            [first[:, :width] - second[:, width:], first[:, width:] + second[:, :width]], axis=1
        )
        p_state = lax.psum(forward_partial_sum, "src") - alpha * u_state
        beta = data_norm(p_state)
        u_state = p_state / beta
        q_state = adjoint(u_state) - beta * v_state
        alpha = model_norm(q_state)
        v_state = q_state / alpha
        rho = jnp.sqrt(rhobar * rhobar + beta * beta)
        cosine = rhobar / rho
        sine = beta / rho
        theta = sine * alpha
        rhobar = -cosine * alpha
        phi = cosine * phibar
        phibar = sine * phibar
        x_state = x_state + phi / rho * w_state
        w_state = v_state - theta / rho * w_state
    factor = math.sqrt(2.0 * lax.axis_size("freq") * cols_local * lax.axis_size("src") * width)
    scaled = w_state * factor
    solution = jnp.stack([x_state[:, :width], x_state[:, width:]])[:, None]
    direction = jnp.stack([scaled[:, :width], scaled[:, width:]])[:, None]
    return (solution, direction)


def solution(mesh):
    return jax.shard_map(
        on_device,
        mesh=mesh,
        in_specs=(P(None, "freq", "rx", "src"), P(None, "freq", "rx", None)),
        out_specs=(P(None, "freq", "src", None), P(None, "freq", "src", None)),
        check_vma=False,
    )
```

profile of v0, /device:TPU:1, one launch (start us, length us, event | category | flops | bytes accessed | tf_op | source)
XLA Modules:
  0.0 984.0 jit_solution(8145905587580802240)
XLA Ops:
  9.3 128.6 %psum.77 = f32[]{:T(128)} all-reduce(f32[]{:T(128)} %multiply_reduce_fusion.5), channel_id=1, replica_groups=mesh['freq'=4,'rx'=16,'src'=4] {'freq','rx'}, use_global_device_ids=true, to_apply=%region_1.0 | all-reduce | flops 1 | bytes 8 | tf_op jit(solution)/shard_map/psum | solution.py:31
  138.7 2.5 fusion.18
  141.5 2.0 fusion.2
  143.6 113.0 %all-reduce.6.cloned.1.call-done = f32[2048,256]{0,1:T(8,128)} async-done(((f32[2048,256]{0,1:T(8,128)}), f32[2048,256]{0,1:T(8,128)}) %all-reduce.6.cloned.1.call-update) | async-done | bytes 2097168 | tf_op jit(solution)/shard_map/psum | solution.py:27
  256.7 2.9 multiply_reduce_fusion.2
  259.6 33.7 %psum.79 = f32[]{:T(128)} all-reduce(f32[]{:T(128)} %multiply_reduce_fusion.2), channel_id=1, replica_groups=mesh['freq'=4,'rx'=16,'src'=4] {'freq','src'}, use_global_device_ids=true, to_apply=%region_4.0 | all-reduce | flops 1 | bytes 8 | tf_op jit(solution)/shard_map/psum | solution.py:36
  294.0 2.5 fusion.20
  298.6 49.2 %all-reduce.8.cloned.1.call-done = f32[512,256]{0,1:T(8,128)} async-done(((f32[512,256]{0,1:T(8,128)}), f32[512,256]{0,1:T(8,128)}) %all-reduce.8.cloned.1.call-update) | async-done | bytes 524304 | tf_op jit(solution)/shard_map/psum | solution.py:56
  349.6 127.0 %psum.81 = f32[]{:T(128)} all-reduce(f32[]{:T(128)} %get-tuple-element.4), channel_id=1, replica_groups=mesh['freq'=4,'rx'=16,'src'=4] {'freq','rx'}, use_global_device_ids=true, to_apply=%region_7.0 | all-reduce | flops 1 | bytes 8 | tf_op jit(solution)/shard_map/psum | solution.py:31
  477.3 2.5 fusion.14
  480.1 2.0 fusion.1
  482.3 110.2 %all-reduce.10.cloned.1.call-done = f32[2048,256]{0,1:T(8,128)} async-done(((f32[2048,256]{0,1:T(8,128)}), f32[2048,256]{0,1:T(8,128)}) %all-reduce.10.cloned.1.call-update) | async-done | bytes 2097168 | tf_op jit(solution)/shard_map/psum | solution.py:27
  592.4 2.7 multiply_reduce_fusion.1
  595.2 33.7 %psum.83 = f32[]{:T(128)} all-reduce(f32[]{:T(128)} %multiply_reduce_fusion.1), channel_id=1, replica_groups=mesh['freq'=4,'rx'=16,'src'=4] {'freq','src'}, use_global_device_ids=true, to_apply=%region_10.0 | all-reduce | flops 1 | bytes 8 | tf_op jit(solution)/shard_map/psum | solution.py:36
  629.6 2.8 broadcast_divide_fusion
  635.6 49.2 %all-reduce.12.cloned.1.call-done = f32[512,256]{0,1:T(8,128)} async-done(((f32[512,256]{0,1:T(8,128)}), f32[512,256]{0,1:T(8,128)}) %all-reduce.12.cloned.1.call-update) | async-done | bytes 524304 | tf_op jit(solution)/shard_map/psum | solution.py:56
  686.6 127.0 %psum.85 = f32[]{:T(128)} all-reduce(f32[]{:T(128)} %multiply_reduce_fusion.3), channel_id=1, replica_groups=mesh['freq'=4,'rx'=16,'src'=4] {'freq','rx'}, use_global_device_ids=true, to_apply=%region_13.0 | all-reduce | flops 1 | bytes 8 | tf_op jit(solution)/shard_map/psum | solution.py:31
  815.5 2.5 fusion.10
  818.3 2.0 fusion
  820.7 109.9 %all-reduce.14.cloned.1.call-done = f32[2048,256]{0,1:T(8,128)} async-done(((f32[2048,256]{0,1:T(8,128)}), f32[2048,256]{0,1:T(8,128)}) %all-reduce.14.cloned.1.call-update) | async-done | bytes 2097168 | tf_op jit(solution)/shard_map/psum | solution.py:27
  930.6 2.7 multiply_reduce_fusion
  933.4 33.7 %psum.87 = f32[]{:T(128)} all-reduce(f32[]{:T(128)} %multiply_reduce_fusion), channel_id=1, replica_groups=mesh['freq'=4,'rx'=16,'src'=4] {'freq','src'}, use_global_device_ids=true, to_apply=%region_16.0 | all-reduce | flops 1 | bytes 8 | tf_op jit(solution)/shard_map/psum | solution.py:36
  967.9 3.0 subtract_multiply_fusion
  972.4 1.8 copy.7
  (45 shorter events, 18.1 us)
Async XLA Ops:
  7.2 249.5 %all-reduce.6.cloned.1.call-start = ((), (), s32[]{:S(2)}) async-start(), calls=%async_computation | async-start | bytes 4194304 | tf_op jit(solution)/shard_map/psum | solution.py:27
  138.7 2.8 copy-start
  143.6 204.2 %all-reduce.8.cloned.1.call-start = ((), (), s32[]{:S(2)}) async-start(), calls=%async_computation.1 | async-start | bytes 1048576 | tf_op jit(solution)/shard_map/psum | solution.py:56
  256.7 37.3 %copy-start.5 = (f32[2048,256]{0,1:T(8,128)S(1)}, f32[2048,256]{0,1:T(8,128)}, u32[]{:S(2)}) copy-start(f32[2048,256]{0,1:T(8,128)} %all-reduce.6.cloned.1.call-done) | copy-start | bytes 6291460
  294.0 2.8 copy-start.1
  298.5 293.9 %all-reduce.10.cloned.1.call-start = ((), (), s32[]{:S(2)}) async-start(), calls=%async_computation.2 | async-start | bytes 4194304 | tf_op jit(solution)/shard_map/psum | solution.py:27
  477.3 2.8 copy-start.2
  482.2 202.6 %all-reduce.12.cloned.1.call-start = ((), (), s32[]{:S(2)}) async-start(), calls=%async_computation.3 | async-start | bytes 1048576 | tf_op jit(solution)/shard_map/psum | solution.py:56
  629.6 3.5 copy-start.3
  635.6 295.1 %all-reduce.14.cloned.1.call-start = ((), (), s32[]{:S(2)}) async-start(), calls=%async_computation.4 | async-start | bytes 4194304 | tf_op jit(solution)/shard_map/psum | solution.py:27
  815.5 2.8 copy-start.4
Sparse Core Ops, SparseCore 0:
  143.7 112.9 all-reduce.5
  298.6 49.1 all-reduce.7
  482.3 110.0 all-reduce.9
  635.7 49.1 all-reduce.11
  820.5 110.0 all-reduce.13
where the time goes:
time: 990 us; the launch traced here: 984 us
  blocking collectives  484 us (49%)
  waiting for transfers between devices  432 us (44%)
  other arithmetic  23.2 us (2%)
  between operations  18.6 us (2%)
  matrix products  18.4 us (2%)
    psum x3, blocking collectives, data_norm(): total = lax.psum(local, ('freq', 'rx'))  383 us
    psum x3, waiting for transfers between devices, adjoint(): return lax.psum(partial_sum, 'rx')  333 us
    psum x3, blocking collectives, model_norm(): total = lax.psum(local, ('freq', 'src'))  101 us
    psum x2, waiting for transfers between devices, on_device(): p_state = lax.psum(forward_partial_sum, 'src') - alpha * u_state  98.4 us
  transfers between devices with their start and end apart: 5, of which 5 were waited for; matrix products, arithmetic and copies ran while one was open for 0% of the time, Pallas kernels for 0%

commit v1 on v0

v1 whole, which is shorter than its diff:
```python
import functools
import math

import jax
import jax.numpy as jnp
from jax import lax
from jax.experimental import pallas as pl
from jax.experimental.pallas import tpu as pltpu
from jax.sharding import PartitionSpec as P

GROUPS = 1
ITERS = 2
PH = ITERS + 1
CH = 256
MESH = pl.DeviceIdType.MESH
F32 = jnp.float32
BF16 = jnp.bfloat16
NN = (((1,), (0,)), ((), ()))
NT = (((1,), (1,)), ((), ()))


def tile_of_squares(x):
    sq = x * x
    rows, lanes = sq.shape
    part = jnp.sum(sq.reshape(rows // 8, 8, lanes), axis=0)
    total = part[:, :128]
    for i in range(1, lanes // 128):
        total = total + part[:, i * 128 : (i + 1) * 128]
    return total


def total_of(tile):
    return jnp.sum(tile, axis=(0, 1), keepdims=True)


def lsqr_kernel(dims, g_hbm, data_ref, q_out, coef_ref, g_v, d_t, p_st, lhs, own, q_prev, acc, sib_s, sib_r, rs_s, rs_r,
                ag, y_s, y_r, nsq, sq_b, sp1_b, sp2_b, g_sem, out_sem, sib_ss, sib_rs, rs_ss, rs_rs, ag_ss, ag_rs,
                as_ss, as_rs, y_ss, y_rs, sq_ss, sq_rs, sp1_ss, sp1_rs, sp2_ss, sp2_rs):
    nx, ny, nz, rows, cols, width = dims
    half = width // 2
    vr = half // GROUPS
    R = 2 * vr
    G = range(GROUPS)
    x = lax.axis_index("freq")
    y = lax.axis_index("src")
    rx = lax.axis_index("rx")
    me = rx // 2
    core = lax.rem(rx, 2)
    sib = {"rx": rx + 1 - 2 * core}

    def zp(off):
        return {"rx": lax.rem(rx + 2 * off + 2 * nz, 2 * nz)}

    def yp(off):
        return {"src": lax.rem(y + off, ny)}

    def chunk(off):
        return lax.rem(me + off + nz, nz)

    started = []

    def rc(src, dst, ss, rs, dev, keep=True):
        c = pltpu.make_async_remote_copy(src_ref=src, dst_ref=dst, send_sem=ss, recv_sem=rs, device_id=dev, device_id_type=MESH)
        c.start()
        if keep:
            started.append(c)

    def wait_recv(dst, ss, rs):
        pltpu.make_async_remote_copy(src_ref=dst, dst_ref=dst, send_sem=ss, recv_sem=rs, device_id=sib, device_id_type=MESH).wait_recv()

    def wait_send(src, ss, rs):
        pltpu.make_async_remote_copy(src_ref=src, dst_ref=src, send_sem=ss, recv_sem=rs, device_id=sib, device_id_type=MESH).wait_send()

    def far_off(t):
        e = lax.rem(t, 2)
        return nz // 2 + (1 - e) * (t // 2) - e * ((t + 1) // 2)

    def g_copy(t):
        ch = chunk(far_off(t))
        lanes = pl.ds(pl.multiple_of(ch * CH, CH), CH)
        return pltpu.make_async_copy(g_hbm.at[:, lanes], g_v.at[:, lanes], g_sem.at[t])

    barrier = pltpu.get_barrier_semaphore()
    peers = [zp(o) for o in range(1, nz)] + [sib]
    xy = [(dx, dy) for dx in range(nx) for dy in range(ny) if dx or dy]

    def xyp(dx, dy):
        return {"freq": lax.rem(x + dx, nx), "src": lax.rem(y + dy, ny)}

    def xcp(dx):
        return {"freq": lax.rem(x + dx, nx), "rx": rx + 1 - 2 * core}

    peers += [xyp(dx, dy) for dx, dy in xy]
    peers += [xcp(dx) for dx in range(1, nx)]
    for t in range(nz):
        g_copy(t).start()
    for p in peers:
        pl.semaphore_signal(barrier, inc=1, device_id=p, device_id_type=MESH)

    for c in range(2):
        d_t[c] = data_ref[c].T
    for g in G:
        for pos in range(2):
            h = core if pos == 0 else 1 - core
            base = pl.multiple_of(h * half + g * vr, vr)
            for c in range(2):
                p_st[g, pos, pl.ds(c * vr, vr), :] = d_t[c, pl.ds(base, vr), :]
    pl.semaphore_wait(barrier, len(peers))

    def sp1_send(k, tile):
        slot = 2 * x + core
        sp1_b[k, slot] = tile
        for i, dev in enumerate([sib] + [f(dx) for dx in range(1, nx) for f in (lambda d: xyp(d, 0), xcp)]):
            rc(sp1_b.at[k, slot], sp1_b.at[k, slot], sp1_ss.at[k, i], sp1_rs.at[k, slot], dev)

    def sp1_wait_sp2_send(k):
        for dx in range(nx):
            for dc in range(2):
                if dx or dc:
                    slot = 2 * lax.rem(x + dx, nx) + lax.rem(core + dc, 2)
                    wait_recv(sp1_b.at[k, slot], sp1_ss.at[k, 0], sp1_rs.at[k, slot])
        tile = sp1_b[k, 0]
        for i in range(1, 2 * nx):
            tile = tile + sp1_b[k, i]
        sp2_b[k, me] = tile
        for i in range(1, nz):
            rc(sp2_b.at[k, me], sp2_b.at[k, me], sp2_ss.at[k, i], sp2_rs.at[k, me], zp(i))

    def sp2_wait(k):
        for i in range(1, nz):
            slot = chunk(i)
            wait_recv(sp2_b.at[k, slot], sp2_ss.at[k, i], sp2_rs.at[k, slot])
        tile = sp2_b[k, 0]
        for i in range(1, nz):
            tile = tile + sp2_b[k, i]
        return jnp.sqrt(total_of(tile))

    def sq_send(k):
        total = None
        for g in G:
            for pos in range(2):
                part = nsq[g, pos, 0]
                for ch in range(1, nz):
                    part = part + nsq[g, pos, ch]
                both = part if pos == 0 else both + part
            total = both if g == 0 else total + both
        slot = x * ny + y
        sq_b[k, slot] = total
        for i, (dx, dy) in enumerate(xy):
            rc(sq_b.at[k, slot], sq_b.at[k, slot], sq_ss.at[k, i], sq_rs.at[k, slot], xyp(dx, dy))

    def sq_wait(k):
        for dx, dy in xy:
            slot = lax.rem(x + dx, nx) * ny + lax.rem(y + dy, ny)
            wait_recv(sq_b.at[k, slot], sq_ss.at[k, 0], sq_rs.at[k, slot])
        tile = sq_b[k, 0]
        for i in range(1, nx * ny):
            tile = tile + sq_b[k, i]
        return jnp.sqrt(total_of(tile))

    def p_norm_tile():
        total = None
        for g in G:
            for pos in range(2):
                t = tile_of_squares(p_st[g, pos])
                total = t if total is None else total + t
        return total

    def a1(k, g):
        for pos in range(2):
            u = p_st[g, pos]
            hi = u.astype(BF16)
            lo = (u - hi.astype(F32)).astype(BF16)
            for i, part in enumerate((hi, lo)):
                r0 = (2 * i + pos) * R
                lhs[g, pl.ds(r0, R), pl.ds(0, rows)] = part
                lhs[g, pl.ds(r0, vr), pl.ds(rows, rows)] = part[vr:]
                lhs[g, pl.ds(r0 + vr, vr), pl.ds(rows, rows)] = -part[:vr]

        def step(t, carry):
            ch = chunk(far_off(t))
            if k == 0 and g == 0:
                g_copy(t).wait()
            lanes = pl.ds(pl.multiple_of(ch * CH, CH), CH)
            res = lax.dot_general(lhs[g], g_v[:, lanes], NN, preferred_element_type=F32)
            both = res[: 2 * R] + res[2 * R :]
            own[g, ch] = both[:R]
            sib_s[k, g, ch] = both[R:]
            rc(sib_s.at[k, g, ch], sib_r.at[k, g, ch], sib_ss.at[k, g, t], sib_rs.at[k, g, t], sib, keep=False)
            return carry

        lax.fori_loop(0, nz, step, 0)

    def a2(k, g):
        def pair(t):
            ch = chunk(far_off(t))
            wait_recv(sib_r.at[k, g, ch], sib_ss.at[k, g, t], sib_rs.at[k, g, t])
            return ch, own[g, ch] + sib_r[k, g, ch]

        def step(t, carry):
            ch, s = pair(t)
            off = far_off(t)
            rs_s[k, g, off] = s.astype(BF16)
            rc(rs_s.at[k, g, off], rs_r.at[k, g, off], rs_ss.at[k, g, off], rs_rs.at[k, g, off], zp(off), keep=False)
            return carry

        lax.fori_loop(0, nz - 1, step, 0)
        ch, s = pair(nz - 1)
        return s

    def a3(k, g, s, inv_beta, coef):
        for off in (1, nz - 1, 2, nz - 2, 3, nz - 3, 4):
            wait_recv(rs_r.at[k, g, off], rs_ss.at[k, g, off], rs_rs.at[k, g, off])
            s = s + rs_r[k, g, off].astype(F32)
        q = s * inv_beta
        if k:
            q = q - coef * q_prev[g]
        q_prev[g] = q
        ag[k, g, 0, me] = q.astype(BF16)
        mine = ag.at[k, g, 0, me]
        for off in (2, nz - 2, 1, nz - 1):
            rel = (nz - off) % nz
            rc(mine, mine, ag_ss.at[k, g, off], ag_rs.at[k, g, rel], zp(off))
        rc(mine, ag.at[k, g, 1, me], as_ss.at[k, g, 0], as_rs.at[k, g, 0], sib)

    def a4(k, g):
        hr = R // 2

        def z_wait(off):
            ch = chunk(off)
            if off == 4:
                wait_recv(ag.at[k, g, 0, ch, pl.ds(0, hr)], ag_ss.at[k, g, 4], ag_rs.at[k, g, 4])
                wait_recv(ag.at[k, g, 0, ch, pl.ds(hr, hr)], ag_ss.at[k, g, 0], ag_rs.at[k, g, 0])
            else:
                wait_recv(ag.at[k, g, 0, ch], ag_ss.at[k, g, off], ag_rs.at[k, g, off])

        def to_sib(off):
            ch = chunk(off)
            rc(ag.at[k, g, 0, ch], ag.at[k, g, 1, ch], as_ss.at[k, g, off], as_rs.at[k, g, off], sib)

        z_wait(2)
        c2 = ag.at[k, g, 0, chunk(2)]
        rc(c2, c2, ag_ss.at[k, g, 3], ag_rs.at[k, g, 3], zp(nz - 1))
        h0 = ag.at[k, g, 0, chunk(2), pl.ds(0, hr)]
        rc(h0, h0, ag_ss.at[k, g, 4], ag_rs.at[k, g, 4], zp(nz - 2))
        z_wait(nz - 2)
        c6 = ag.at[k, g, 0, chunk(nz - 2)]
        rc(c6, c6, ag_ss.at[k, g, 5], ag_rs.at[k, g, 5], zp(1))
        h1 = ag.at[k, g, 0, chunk(nz - 2), pl.ds(hr, hr)]
        rc(h1, h1, ag_ss.at[k, g, 0], ag_rs.at[k, g, 0], zp(2))
        to_sib(2)
        to_sib(nz - 2)
        for off in (1, nz - 1, 3, nz - 3, 4):
            z_wait(off)
            to_sib(off)

    order = (0, 2, nz - 2, 1, nz - 1, 3, nz - 3, 4)

    def sib_wait(k, g, off):
        wait_recv(ag.at[k, g, 1, chunk(off)], as_ss.at[k, g, off], as_rs.at[k, g, off])

    def f1(k, g):
        for n, off in enumerate(order):
            ch = chunk(off)
            sib_wait(k, g, off)
            lanes = pl.ds(pl.multiple_of(ch * CH, CH), CH)
            v0 = ag[k, g, 0, ch]
            v1 = ag[k, g, 1, ch]
            v = jnp.concatenate([v0, v1], axis=0)
            w = jnp.concatenate([-v0[vr:], v0[:vr], -v1[vr:], v1[:vr]], axis=0)
            res = lax.dot_general(v, g_v[pl.ds(0, rows), lanes], NT, preferred_element_type=F32)
            res = res + lax.dot_general(w, g_v[pl.ds(rows, rows), lanes], NT, preferred_element_type=F32)
            if n == 0:
                acc[g] = res
            else:
                acc[g] += res
        y_s[k, g] = acc[g].astype(BF16)
        for off in (2, 1, 3):
            rc(y_s.at[k, g], y_r.at[k, g, off], y_ss.at[k, g, off], y_rs.at[k, g, off], yp(off))

    def q_norms(k, g):
        for pos in range(2):
            for ch in range(nz):
                nsq[g, pos, ch] = tile_of_squares(ag[k, g, pos, ch].astype(F32))

    def f2(k, g, inv_alpha, coef):
        for off in (1, 3, 2):
            wait_recv(y_r.at[k, g, off], y_ss.at[k, g, off], y_rs.at[k, g, off])
        for pos in range(2):
            sl = pl.ds(pos * R, R)
            s = acc[g, sl]
            for off in (1, 2, 3):
                s = s + y_r[k, g, off, sl].astype(F32)
            p_st[g, pos] = s * inv_alpha - coef * p_st[g, pos]

    def out_copy(k):
        return pltpu.make_async_copy(ag.at[k], q_out.at[k], out_sem.at[k])

    alphas, betas = [], []
    for k in range(PH):
        sp1_send(k, p_norm_tile())
        for g in G:
            a1(k, g)
        sp1_wait_sp2_send(k)
        sums = [a2(k, g) for g in G]
        beta = sp2_wait(k)
        betas.append(beta)
        inv_beta = 1.0 / beta
        for g in G:
            a3(k, g, sums[g], inv_beta, beta / alphas[-1] if k else None)
        for g in G:
            a4(k, g)
        if k < ITERS:
            for g in G:
                f1(k, g)
            for g in G:
                q_norms(k, g)
            sq_send(k)
            out_copy(k).start()
            alpha = sq_wait(k)
            alphas.append(alpha)
            for g in G:
                f2(k, g, 1.0 / alpha, alpha / beta)
        else:
            for g in G:
                for off in order:
                    sib_wait(k, g, off)
                q_norms(k, g)
            sq_send(k)
            out_copy(k).start()
            alphas.append(sq_wait(k))

    factor = math.sqrt(2.0 * nx * cols * ny * width)
    phibar, rhobar = betas[0], alphas[0]
    x_w = [None] * PH
    w_w = [1.0 / alphas[0]] + [None] * ITERS
    for it in range(ITERS):
        beta, alpha = betas[it + 1], alphas[it + 1]
        rho = jnp.sqrt(rhobar * rhobar + beta * beta)
        cosine, sine = rhobar / rho, beta / rho
        theta = sine * alpha
        rhobar = -cosine * alpha
        phi = cosine * phibar
        phibar = sine * phibar
        step, back = phi / rho, theta / rho
        for j in range(it + 1):
            x_w[j] = step * w_w[j] if x_w[j] is None else x_w[j] + step * w_w[j]
            w_w[j] = -back * w_w[j]
        w_w[it + 1] = 1.0 / alpha
    for j in range(ITERS):
        coef_ref[j] = jnp.broadcast_to(x_w[j], (8, 128))
    for j in range(PH):
        coef_ref[ITERS + j] = jnp.broadcast_to(w_w[j] * factor, (8, 128))

    for k in range(PH):
        out_copy(k).wait()
    for c in started:
        c.wait_send()
    for k in range(PH):
        for g in G:
            def fin(t, carry, k=k, g=g):
                wait_send(sib_s.at[k, g, t], sib_ss.at[k, g, t], sib_rs.at[k, g, t])
                return carry
            lax.fori_loop(0, nz, fin, 0)

            def fin2(t, carry, k=k, g=g):
                wait_send(rs_s.at[k, g, t], rs_ss.at[k, g, t], rs_rs.at[k, g, t])
                return carry
            lax.fori_loop(1, nz, fin2, 0)


def finish_kernel(dims, q_ref, coef_ref, x_ref, w_ref, buf):
    nx, ny, nz, rows, cols, width = dims
    half = width // 2
    vr = half // GROUPS
    core = lax.rem(lax.axis_index("rx"), 2)
    cf = [coef_ref[j, 0:1, 0:1] for j in range(ITERS + PH)]
    for g in range(GROUPS):
        for pos in range(2):
            h = core if pos == 0 else 1 - core
            base = pl.multiple_of(h * half + g * vr, vr)
            q = [q_ref[k, g, pos, 0].astype(F32) for k in range(PH)]
            xv = cf[0] * q[0]
            for j in range(1, ITERS):
                xv = xv + cf[j] * q[j]
            wv = cf[ITERS] * q[0]
            for j in range(1, PH):
                wv = wv + cf[ITERS + j] * q[j]
            for c in range(2):
                buf[0, c, pl.ds(base, vr), :] = xv[c * vr : (c + 1) * vr]
                buf[1, c, pl.ds(base, vr), :] = wv[c * vr : (c + 1) * vr]
    for c in range(2):
        x_ref[c, 0] = buf[0, c].T
        w_ref[c, 0] = buf[1, c].T


def on_device(nx, ny, nz, kernel, data):
    rows, cols, width = kernel.shape[2], kernel.shape[3], data.shape[3]
    dims = (nx, ny, nz, rows, cols, width)
    R = width // GROUPS
    G = GROUPS
    sem = pltpu.SemaphoreType.DMA
    vm = pltpu.VMEM
    q_all, coefs = pl.pallas_call(
        functools.partial(lsqr_kernel, dims),
        name="lsqr",
        out_shape=(
            jax.ShapeDtypeStruct((PH, G, 2, nz, R, CH), BF16),
            jax.ShapeDtypeStruct((ITERS + PH, 8, 128), F32),
        ),
        in_specs=[pl.BlockSpec(memory_space=pl.ANY), pl.BlockSpec(memory_space=pltpu.VMEM)],
        out_specs=(pl.BlockSpec(memory_space=pl.ANY), pl.BlockSpec(memory_space=pltpu.VMEM)),
        scratch_shapes=[
            vm((2 * rows, cols), BF16),
            vm((2, width, rows), F32),
            vm((G, 2, R, rows), F32),
            vm((G, 4 * R, 2 * rows), BF16),
            vm((G, nz, R, CH), F32),
            vm((G, R, CH), F32),
            vm((G, 2 * R, rows), F32),
            vm((PH, G, nz, R, CH), F32),
            vm((PH, G, nz, R, CH), F32),
            vm((PH, G, nz, R, CH), BF16),
            vm((PH, G, nz, R, CH), BF16),
            vm((PH, G, 2, nz, R, CH), BF16),
            vm((ITERS, G, 2 * R, rows), BF16),
            vm((ITERS, G, ny, 2 * R, rows), BF16),
            vm((G, 2, nz, 8, 128), F32),
            vm((PH, nx * ny, 8, 128), F32),
            vm((PH, 2 * nx, 8, 128), F32),
            vm((PH, nz, 8, 128), F32),
            sem((nz,)),
            sem((PH,)),
            sem((PH, G, nz)), sem((PH, G, nz)),
            sem((PH, G, nz)), sem((PH, G, nz)),
            sem((PH, G, nz)), sem((PH, G, nz)),
            sem((PH, G, nz)), sem((PH, G, nz)),
            sem((ITERS, G, ny)), sem((ITERS, G, ny)),
            sem((PH, nx * ny)), sem((PH, nx * ny)),
            sem((PH, 2 * nx)), sem((PH, 2 * nx)),
            sem((PH, nz)), sem((PH, nz)),
        ],
        compiler_params=pltpu.CompilerParams(collective_id=0, has_side_effects=True, vmem_limit_bytes=56 << 20),
    )(kernel.reshape(2 * rows, cols), data[:, 0])
    out = jax.ShapeDtypeStruct((2, 1, cols, width), F32)
    return pl.pallas_call(
        functools.partial(finish_kernel, dims),
        name="finish",
        grid=(nz,),
        out_shape=(out, out),
        in_specs=[
            pl.BlockSpec((PH, G, 2, 1, R, CH), lambda i: (0, 0, 0, i, 0, 0)),
            pl.BlockSpec((ITERS + PH, 8, 128), lambda i: (0, 0, 0)),
        ],
        out_specs=(
            pl.BlockSpec((2, 1, CH, width), lambda i: (0, 0, i, 0)),
            pl.BlockSpec((2, 1, CH, width), lambda i: (0, 0, i, 0)),
        ),
        scratch_shapes=[vm((2, 2, width, CH), F32)],
    )(q_all, coefs)


def solution(mesh):
    nx, ny, nz = mesh.shape["freq"], mesh.shape["src"], mesh.shape["rx"] // 2
    return jax.shard_map(
        functools.partial(on_device, nx, ny, nz),
        mesh=mesh,
        in_specs=(P(None, "freq", "rx", "src"), P(None, "freq", "rx", None)),
        out_specs=(P(None, "freq", "src", None), P(None, "freq", "src", None)),
        check_vma=False,
    )
```

time: 990 us -> 149 us (0.15)
  blocking collectives: 484 us -> 0 us
  waiting for transfers between devices: 432 us -> 0 us
  Pallas kernels: 0 us -> 148 us
  other arithmetic: 23.2 us -> 0 us
  matrix products: 18.4 us -> 0 us
  between operations: 18.6 us -> 0.64 us
    psum x6 -> x0, blocking collectives: 484 us -> none  [the longest x3 383 us: data_norm(): total = lax.psum(local, ('freq', 'rx'))]
    psum x5 -> x0, waiting for transfers between devices: 432 us -> none  [the longest x3 333 us: adjoint(): return lax.psum(partial_sum, 'rx')]
    pallas_call x0 -> x2, Pallas kernels: none -> 148 us  [the longest x1 141 us: on_device(): pl.pallas_call(functools.partial(lsqr_kernel, dims), name='lsqr', out_sha...]
    dot_general x10 -> x0, matrix products: 18.4 us -> none  [the longest x3 7.43 us: adjoint_term(): lax.dot_general(real_part, piece, dims, preferred_element_type=jnp.float32)]
    reduce_sum x6 -> x0, other arithmetic: 12.7 us -> none  [the longest x3 8.36 us: model_norm(): local = jnp.sum(field * field)]
  transfers between devices with their start and end apart: 5 -> 0, of which waited for: 5 -> 0; matrix products, arithmetic and copies ran while one was open for 0% -> 0% of each run, Pallas kernels for 0% -> 0%
where the time goes in v1:
time: 149 us
  Pallas kernels  148 us (99%)
    pallas_call x1, Pallas kernels, on_device(): pl.pallas_call(functools.partial(lsqr_kernel, dims), name='lsqr', out_sha...  141 us
    pallas_call x1, Pallas kernels, on_device(): pl.pallas_call(functools.partial(finish_kernel, dims), name='finish', gri...  7.58 us

profile of v1, /device:TPU:1, one launch (start us, length us, event | category | flops | bytes accessed | tf_op | source)
XLA Modules:
  0.0 148.9 jit_solution(3977136165656574850)
XLA Ops:
  0.6 140.6 %lsqr.1 = (bf16[3,1,2,8,128,256]{5,4,3,2,1,0:T(8,128)(2,1)}, f32[5,8,128]{2,1,0:T(8,128)}) custom-call(bf16[1024,2048]{1,0:T(8,128)(2,1)} %bitcast.2, f32[2,512,128]{2,1,0:T(8,128)} %bitcast.3), custom_call_target="tpu_custom_call" | custom-call | tf_op jit(solution)/shard_map/lsqr/pallas_call | solution.py:404
  141.3 7.6 %finish.1 = (f32[2,1,2048,128]{3,2,1,0:T(8,128)}, f32[2,1,2048,128]{3,2,1,0:T(8,128)}) custom-call(bf16[3,1,2,8,128,256]{5,4,3,2,1,0:T(8,128)(2,1)} %get-tuple-element.4.q_ref, f32[5,8,128]{2,1,0:T(8,128)} %get-tuple-element.5.coef_ref), custom_call_target="tpu_custom_call" | custom-call | tf_op jit(solution)/shard_map/finish/pallas_call | solution.py:446

commit v2 on v0

v2 whole, which is shorter than its diff:
```python
import functools
import math

import jax
import jax.numpy as jnp
from jax import lax
from jax.experimental import pallas as pl
from jax.experimental.pallas import tpu as pltpu
from jax.sharding import PartitionSpec as P

GROUPS = 1
ITERS = 2
PH = ITERS + 1
CH = 256
MESH = pl.DeviceIdType.MESH
F32 = jnp.float32
BF16 = jnp.bfloat16
NN = (((1,), (0,)), ((), ()))
NT = (((1,), (1,)), ((), ()))


def tile_of_squares(x):
    sq = x * x
    rows, lanes = sq.shape
    part = jnp.sum(sq.reshape(rows // 8, 8, lanes), axis=0)
    total = part[:, :128]
    for i in range(1, lanes // 128):
        total = total + part[:, i * 128 : (i + 1) * 128]
    return total


def total_of(tile):
    return jnp.sum(tile, axis=(0, 1), keepdims=True)


FAR = (4, 3, 5, 2, 6, 1, 7, 0)
BATCHES = ((0, 2), (2, 3), (3, 5), (5, 8))
HILO = (True, True, False)


def lsqr_kernel(dims, g_hbm, data_hbm, q_out, coef_ref, g_v, data_ref, d_t, p_st, lhs, own, q_prev, acc, sib_s, sib_r, rs_s, rs_r,
                ag, y_s, y_r, nsq, sq_b, sp1_b, sp2_b, zc_b, g_sem, out_sem, sib_ss, sib_rs, rs_ss, rs_rs, ag_ss, ag_rs,
                as_ss, as_rs, y_ss, y_rs, sq_ss, sq_rs, sp1_ss, sp1_rs, sp2_ss, sp2_rs, zc_ss, zc_rs):
    nx, ny, nz, rows, cols, width = dims
    half = width // 2
    vr = half // GROUPS
    R = 2 * vr
    hr = R // 2
    G = range(GROUPS)
    x = lax.axis_index("freq")
    y = lax.axis_index("src")
    rx = lax.axis_index("rx")
    me = rx // 2
    core = lax.rem(rx, 2)
    sib = {"rx": rx + 1 - 2 * core}
    zps = [{"rx": lax.rem(rx + 2 * o, 2 * nz)} for o in range(nz)]
    zcs = [{"rx": lax.rem(rx + 2 * o, 2 * nz) + 1 - 2 * core} for o in range(nz)]
    ynb = [{"src": y + 1 - 2 * lax.rem(y, 2)}, {"src": ny - 1 - y}]
    xps = [{"freq": lax.rem(x + o, nx)} for o in range(nx)]
    xcs = [{"freq": lax.rem(x + o, nx), "rx": rx + 1 - 2 * core} for o in range(nx)]
    xy = [(dx, dy) for dx in range(nx) for dy in range(ny) if dx or dy]
    xys = [{"freq": lax.rem(x + dx, nx), "src": lax.rem(y + dy, ny)} for dx, dy in xy]
    chunks = [lax.rem(me + o, nz) for o in range(nz)]
    lanes = [pl.ds(pl.multiple_of(c * CH, CH), CH) for c in chunks]

    started = []

    def rc(src, dst, ss, rs, dev):
        c = pltpu.make_async_remote_copy(src_ref=src, dst_ref=dst, send_sem=ss, recv_sem=rs, device_id=dev, device_id_type=MESH)
        c.start()
        started.append(c)

    def drain():
        for c in started:
            c.wait_send()
        started.clear()

    def wait_recv(dst, ss, rs):
        pltpu.make_async_remote_copy(src_ref=dst, dst_ref=dst, send_sem=ss, recv_sem=rs, device_id=sib, device_id_type=MESH).wait_recv()

    def g_copy(t):
        sl = lanes[FAR[t]]
        return pltpu.make_async_copy(g_hbm.at[:, sl], g_v.at[:, sl], g_sem.at[t])

    barrier = pltpu.get_barrier_semaphore()
    peers = zps[1:] + zcs + xys + xcs[1:]
    data_copy = pltpu.make_async_copy(data_hbm, data_ref, g_sem.at[nz])
    data_copy.start()
    for t in range(nz):
        g_copy(t).start()
    for p in peers:
        pl.semaphore_signal(barrier, inc=1, device_id=p, device_id_type=MESH)

    def tiles_send(buf, slot, tile, ss, rs, devs):
        buf[slot] = tile
        for i, dev in enumerate(devs):
            rc(buf.at[slot], buf.at[slot], ss.at[i], rs.at[slot], dev)

    def tiles_wait(buf, n, slots, ss, rs):
        for slot in slots:
            wait_recv(buf.at[slot], ss.at[0], rs.at[slot])
        tile = buf[0]
        for i in range(1, n):
            tile = tile + buf[i]
        return tile

    def sp1_send(k):
        tile = None
        for g in G:
            for pos in range(2):
                t = tile_of_squares(p_st[g, pos])
                tile = t if tile is None else tile + t
        tiles_send(sp1_b.at[k], 2 * x + core, tile, sp1_ss.at[k], sp1_rs.at[k], [sib] + xps[1:] + xcs[1:])

    def sp1_wait_sp2_send(k):
        slots = [2 * lax.rem(x + dx, nx) + lax.rem(core + dc, 2) for dx in range(nx) for dc in range(2) if dx or dc]
        tile = tiles_wait(sp1_b.at[k], 2 * nx, slots, sp1_ss.at[k], sp1_rs.at[k])
        tiles_send(sp2_b.at[k], me, tile, sp2_ss.at[k], sp2_rs.at[k], zps[1:])

    def sp2_wait(k):
        return jnp.sqrt(total_of(tiles_wait(sp2_b.at[k], nz, chunks[1:], sp2_ss.at[k], sp2_rs.at[k])))

    def sq_send(k):
        total = None
        for g in G:
            for pos in range(2):
                part = nsq[g, pos, 0]
                for ch in range(1, nz):
                    part = part + nsq[g, pos, ch]
                both = part if pos == 0 else both + part
            total = both if g == 0 else total + both
        tiles_send(sq_b.at[k], x * ny + y, total, sq_ss.at[k], sq_rs.at[k], xys)

    def sq_tile(k):
        slots = [lax.rem(x + dx, nx) * ny + lax.rem(y + dy, ny) for dx, dy in xy]
        return tiles_wait(sq_b.at[k], nx * ny, slots, sq_ss.at[k], sq_rs.at[k])

    def last_norm_send(k):
        total = None
        for g in G:
            t = tile_of_squares(ag[k, g, 0, 0].astype(F32))
            total = t if total is None else total + t
        tiles_send(sq_b.at[k], x * ny + y, total, sq_ss.at[k], sq_rs.at[k], xys)

    def last_norm_mid(k):
        tiles_send(zc_b, rx, sq_tile(k), zc_ss, zc_rs, zcs + zps[1:])

    def last_norm_wait():
        slots = [lax.rem(rx + d, 2 * nz) for d in range(1, 2 * nz)]
        return jnp.sqrt(total_of(tiles_wait(zc_b, 2 * nz, slots, zc_ss, zc_rs)))

    def build(k, g):
        for pos in range(2):
            u = p_st[g, pos]
            hi = u.astype(BF16)
            parts = (hi, (u - hi.astype(F32)).astype(BF16)) if HILO[k] else (hi,)
            for i, part in enumerate(parts):
                r0 = (2 * i + pos) * R
                lhs[g, r0 : r0 + R, :rows] = part
                lhs[g, r0 : r0 + vr, rows:] = part[vr:]
                lhs[g, r0 + vr : r0 + R, rows:] = -part[:vr]

    def a1(k, g, batch):
        for t in range(*BATCHES[batch]):
            if k == 0 and g == 0:
                g_copy(t).wait()
            if HILO[k]:
                res = lax.dot_general(lhs[g], g_v[:, lanes[FAR[t]]], NN, preferred_element_type=F32)
                both = res[: 2 * R] + res[2 * R :]
            else:
                both = lax.dot_general(lhs[g, : 2 * R], g_v[:, lanes[FAR[t]]], NN, preferred_element_type=F32)
            own[g, t] = both[:R]
            sib_s[k, g, t] = both[R:]
        t0, t1 = BATCHES[batch]
        part = pl.ds(t0, t1 - t0)
        rc(sib_s.at[k, g, part], sib_r.at[k, g, part], sib_ss.at[k, g, batch], sib_rs.at[k, g, batch], sib)

    def rs_send(k, g, slot, to, lo=0, n=R):
        part = pl.ds(lo, n)
        rc(rs_s.at[k, g, slot, part], rs_r.at[k, g, slot, part], rs_ss.at[k, g, slot], rs_rs.at[k, g, slot], zps[to])

    def rs_wait(k, g, slot, lo=0, n=R):
        part = pl.ds(lo, n)
        wait_recv(rs_r.at[k, g, slot, part], rs_ss.at[k, g, slot], rs_rs.at[k, g, slot])

    def a2(k, g, batch):
        t0, t1 = BATCHES[batch]
        part = pl.ds(t0, t1 - t0)
        wait_recv(sib_r.at[k, g, part], sib_ss.at[k, g, batch], sib_rs.at[k, g, batch])
        for t in range(t0, t1):
            off = FAR[t]
            pair = own[g, t] + sib_r[k, g, t]
            if off == 4:
                rs_s[k, g, 4, :hr] = pair[:hr].astype(BF16)
                rs_s[k, g, 0, hr:] = pair[hr:].astype(BF16)
                rs_send(k, g, 4, 2, 0, hr)
                rs_send(k, g, 0, nz - 2, hr, hr)
            elif off in (0, 2, nz - 2):
                own[g, t] = pair
            else:
                rs_s[k, g, off] = pair.astype(BF16)
                rs_send(k, g, off, 1 if off in (1, 3) else nz - 1)

    def a2b(k, g):
        rs_wait(k, g, 3)
        rs_wait(k, g, 4, 0, hr)
        s = own[g, FAR.index(2)] + rs_r[k, g, 3].astype(F32)
        rs_s[k, g, 2, :hr] = (s[:hr] + rs_r[k, g, 4, :hr].astype(F32)).astype(BF16)
        rs_s[k, g, 2, hr:] = s[hr:].astype(BF16)
        rs_send(k, g, 2, 2)
        rs_wait(k, g, nz - 3)
        rs_wait(k, g, 0, hr, hr)
        s = own[g, FAR.index(nz - 2)] + rs_r[k, g, nz - 3].astype(F32)
        rs_s[k, g, nz - 2, :hr] = s[:hr].astype(BF16)
        rs_s[k, g, nz - 2, hr:] = (s[hr:] + rs_r[k, g, 0, hr:].astype(F32)).astype(BF16)
        rs_send(k, g, nz - 2, nz - 2)

    def ag_send(k, g, rel, to, lo=0, n=R, sem=None):
        there = (rel - to) % nz
        sem = there if sem is None else sem
        rc(ag.at[k, g, 0, rel, pl.ds(lo, n)], ag.at[k, g, 0, there, pl.ds(lo, n)], ag_ss.at[k, g, sem], ag_rs.at[k, g, sem], zps[to])

    def z_wait(k, g, rel):
        if rel == 4:
            wait_recv(ag.at[k, g, 0, 4, pl.ds(0, hr)], ag_ss.at[k, g, 4], ag_rs.at[k, g, 4])
            wait_recv(ag.at[k, g, 0, 4, pl.ds(hr, hr)], ag_ss.at[k, g, 0], ag_rs.at[k, g, 0])
        else:
            wait_recv(ag.at[k, g, 0, rel], ag_ss.at[k, g, rel], ag_rs.at[k, g, rel])

    def to_sib(k, g, rel, n=1):
        part = pl.ds(rel, n)
        rc(ag.at[k, g, 0, part], ag.at[k, g, 1, part], as_ss.at[k, g, rel], as_rs.at[k, g, rel], sib)

    def sib_wait(k, g, rel, n=1):
        part = pl.ds(rel, n)
        wait_recv(ag.at[k, g, 1, part], as_ss.at[k, g, rel], as_rs.at[k, g, rel])

    def a3(k, g, inv_beta, coef):
        s = own[g, FAR.index(0)]
        for off in (1, nz - 1, 2, nz - 2):
            rs_wait(k, g, off)
            s = s + rs_r[k, g, off].astype(F32)
        q = s * inv_beta
        if k:
            q = q - coef * q_prev[g]
        q_prev[g] = q
        ag[k, g, 0, 0] = q.astype(BF16)
        for to in (2, nz - 2, 1, nz - 1):
            ag_send(k, g, 0, to)
        to_sib(k, g, 0)

    def a4a(k, g):
        z_wait(k, g, 2)
        ag_send(k, g, 2, nz - 1)
        ag_send(k, g, 2, nz - 2, 0, hr, 4)
        z_wait(k, g, nz - 2)
        ag_send(k, g, nz - 2, 1)
        ag_send(k, g, nz - 2, 2, hr, hr, 0)
        z_wait(k, g, 1)
        to_sib(k, g, 1, 2)
        z_wait(k, g, nz - 1)
        to_sib(k, g, nz - 2, 2)

    def a4b(k, g):
        for rel in (3, nz - 3, 4):
            z_wait(k, g, rel)
            to_sib(k, g, rel)

    def f1(k, g, rel):
        v0 = ag[k, g, 0, rel]
        v1 = ag[k, g, 1, rel]
        v = jnp.concatenate([v0, v1], axis=0)
        w = jnp.concatenate([-v0[vr:], v0[:vr], -v1[vr:], v1[:vr]], axis=0)
        res = lax.dot_general(v, g_v[:rows, lanes[rel]], NT, preferred_element_type=F32)
        res = res + lax.dot_general(w, g_v[rows:, lanes[rel]], NT, preferred_element_type=F32)
        if rel == 0:
            acc[g] = res
        else:
            acc[g] += res

    def q_norms(k, g, rel):
        for pos in range(2):
            nsq[g, pos, chunks[rel]] = tile_of_squares(ag[k, g, pos, rel].astype(F32))

    YP = [(pos, slice(pos * R + n * hr, pos * R + n * hr + hr), 2 * n + pos) for n in range(2) for pos in range(2)]

    def y_send(k, g, step):
        for pos, sl, i in YP:
            if step:
                wait_recv(y_r.at[k, g, 0, sl], y_ss.at[k, g, 0, i], y_rs.at[k, g, 0, i])
                acc[g, sl] = acc[g, sl] + y_r[k, g, 0, sl].astype(F32)
            y_s[k, g, step, sl] = acc[g, sl].astype(BF16)
            dev = ynb[(pos + step) % 2]
            rc(y_s.at[k, g, step, sl], y_r.at[k, g, step, sl], y_ss.at[k, g, step, i], y_rs.at[k, g, step, i], dev)

    def f2(k, g, inv_alpha, coef):
        for pos, sl, i in YP:
            wait_recv(y_r.at[k, g, 1, sl], y_ss.at[k, g, 1, i], y_rs.at[k, g, 1, i])
            total = acc[g, sl] + y_r[k, g, 1, sl].astype(F32)
            rs = slice(sl.start - pos * R, sl.stop - pos * R)
            p_st[g, pos, rs] = total * inv_alpha - coef * p_st[g, pos, rs]

    def out_copy(k):
        return pltpu.make_async_copy(ag.at[k], q_out.at[k], out_sem.at[k])

    data_copy.wait()
    for c in range(2):
        d_t[c] = data_ref[c].T
    for g in G:
        for pos in range(2):
            h = core if pos == 0 else 1 - core
            base = pl.multiple_of(h * half + g * vr, vr)
            for c in range(2):
                p_st[g, pos, c * vr : (c + 1) * vr, :] = d_t[c, pl.ds(base, vr), :]
    build(0, 0)
    pl.semaphore_wait(barrier, len(peers))

    alphas, betas = [], []
    for k in range(PH):
        last = k == ITERS
        for g in G:
            if k:
                f2(k - 1, g, inv_alpha, alphas[-1] / betas[-1])
            if k or g:
                build(k, g)
            a1(k, g, 0)
            a1(k, g, 1)
            if g == GROUPS - 1:
                sp1_send(k)
            a2(k, g, 0)
            a2(k, g, 1)
            a1(k, g, 2)
        for g in G:
            a1(k, g, 3)
            a2(k, g, 2)
            a2(k, g, 3)
        sp1_wait_sp2_send(k)
        for g in G:
            a2b(k, g)
        betas.append(sp2_wait(k))
        inv_beta = 1.0 / betas[-1]
        coef = betas[-1] / alphas[-1] if k else None
        for g in G:
            a3(k, g, inv_beta, coef)
        if last:
            last_norm_send(k)
            for g in G:
                a4a(k, g)
            last_norm_mid(k)
            for g in G:
                a4b(k, g)
            drain()
            for g in G:
                for rel, n in ((0, 1), (1, 2), (nz - 2, 2), (3, 1), (nz - 3, 1), (4, 1)):
                    sib_wait(k, g, rel, n)
            out_copy(k).start()
            alphas.append(last_norm_wait())
            break
        for g in G:
            sib_wait(k, g, 0)
            f1(k, g, 0)
        for g in G:
            a4a(k, g)
        for g in G:
            sib_wait(k, g, 1, 2)
            f1(k, g, 1)
            f1(k, g, 2)
            sib_wait(k, g, nz - 2, 2)
            f1(k, g, nz - 2)
            f1(k, g, nz - 1)
        for g in G:
            for rel in (0, 1, 2, nz - 2, nz - 1):
                q_norms(k, g, rel)
        for g in G:
            a4b(k, g)
        for g in G:
            for rel in (3, nz - 3, 4):
                sib_wait(k, g, rel)
                f1(k, g, rel)
            y_send(k, g, 0)
        for g in G:
            for rel in (3, nz - 3, 4):
                q_norms(k, g, rel)
        sq_send(k)
        out_copy(k).start()
        for g in G:
            y_send(k, g, 1)
        drain()
        alphas.append(jnp.sqrt(total_of(sq_tile(k))))
        inv_alpha = 1.0 / alphas[-1]

    factor = math.sqrt(2.0 * nx * cols * ny * width)
    phibar, rhobar = betas[0], alphas[0]
    x_w = [None] * PH
    w_w = [1.0 / alphas[0]] + [None] * ITERS
    for it in range(ITERS):
        beta, alpha = betas[it + 1], alphas[it + 1]
        rho = jnp.sqrt(rhobar * rhobar + beta * beta)
        cosine, sine = rhobar / rho, beta / rho
        theta = sine * alpha
        rhobar = -cosine * alpha
        phi = cosine * phibar
        phibar = sine * phibar
        step, back = phi / rho, theta / rho
        for j in range(it + 1):
            x_w[j] = step * w_w[j] if x_w[j] is None else x_w[j] + step * w_w[j]
            w_w[j] = -back * w_w[j]
        w_w[it + 1] = 1.0 / alpha
    for j in range(ITERS):
        coef_ref[j] = jnp.broadcast_to(x_w[j], (8, 128))
    for j in range(PH):
        coef_ref[ITERS + j] = jnp.broadcast_to(w_w[j] * factor, (8, 128))

    for k in range(PH):
        out_copy(k).wait()


FIN = 4


def finish_kernel(dims, *refs):
    nx, ny, nz, rows, cols, width = dims
    q_refs, (coef_ref, x_ref, w_ref, buf) = refs[:FIN], refs[FIN:]
    half = width // 2
    vr = half // GROUPS
    core = lax.rem(lax.axis_index("rx"), 2)
    cf = [coef_ref[j, 0:1, 0:1] for j in range(ITERS + PH)]
    for n, q_ref in enumerate(q_refs):
        for g in range(GROUPS):
            for pos in range(2):
                h = core if pos == 0 else 1 - core
                base = pl.multiple_of(h * half + g * vr, vr)
                q = [q_ref[k, g, pos, 0].astype(F32) for k in range(PH)]
                xv = cf[0] * q[0]
                for j in range(1, ITERS):
                    xv = xv + cf[j] * q[j]
                wv = cf[ITERS] * q[0]
                for j in range(1, PH):
                    wv = wv + cf[ITERS + j] * q[j]
                for c in range(2):
                    buf[n, 0, c, pl.ds(base, vr), :] = xv[c * vr : (c + 1) * vr]
                    buf[n, 1, c, pl.ds(base, vr), :] = wv[c * vr : (c + 1) * vr]
        for c in range(2):
            x_ref[c, 0, n * CH : (n + 1) * CH] = buf[n, 0, c].T
            w_ref[c, 0, n * CH : (n + 1) * CH] = buf[n, 1, c].T


def on_device(nx, ny, nz, kernel, data):
    rows, cols, width = kernel.shape[2], kernel.shape[3], data.shape[3]
    dims = (nx, ny, nz, rows, cols, width)
    R = width // GROUPS
    G = GROUPS
    sem = pltpu.SemaphoreType.DMA
    vm = pltpu.VMEM
    q_all, coefs = pl.pallas_call(
        functools.partial(lsqr_kernel, dims),
        name="lsqr",
        out_shape=(
            jax.ShapeDtypeStruct((PH, G, 2, nz, R, CH), BF16),
            jax.ShapeDtypeStruct((ITERS + PH, 8, 128), F32),
        ),
        in_specs=[pl.BlockSpec(memory_space=pl.ANY), pl.BlockSpec(memory_space=pl.ANY)],
        out_specs=(pl.BlockSpec(memory_space=pl.ANY), pl.BlockSpec(memory_space=pltpu.VMEM)),
        scratch_shapes=[
            vm((2 * rows, cols), BF16),
            vm((2, rows, width), F32),
            vm((2, width, rows), F32),
            vm((G, 2, R, rows), F32),
            vm((G, 4 * R, 2 * rows), BF16),
            vm((G, nz, R, CH), F32),
            vm((G, R, CH), F32),
            vm((G, 2 * R, rows), F32),
            vm((PH, G, nz, R, CH), F32),
            vm((PH, G, nz, R, CH), F32),
            vm((PH, G, nz, R, CH), BF16),
            vm((PH, G, nz, R, CH), BF16),
            vm((PH, G, 2, nz, R, CH), BF16),
            vm((ITERS, G, 2, 2 * R, rows), BF16),
            vm((ITERS, G, 2, 2 * R, rows), BF16),
            vm((G, 2, nz, 8, 128), F32),
            vm((PH, nx * ny, 8, 128), F32),
            vm((PH, 2 * nx, 8, 128), F32),
            vm((PH, nz, 8, 128), F32),
            vm((2 * nz, 8, 128), F32),
            sem((nz + 1,)),
            sem((PH,)),
            sem((PH, G, nz)), sem((PH, G, nz)),
            sem((PH, G, nz)), sem((PH, G, nz)),
            sem((PH, G, nz)), sem((PH, G, nz)),
            sem((PH, G, nz)), sem((PH, G, nz)),
            sem((ITERS, G, 2, 4)), sem((ITERS, G, 2, 4)),
            sem((PH, nx * ny)), sem((PH, nx * ny)),
            sem((PH, 2 * nx)), sem((PH, 2 * nx)),
            sem((PH, nz)), sem((PH, nz)),
            sem((2 * nz,)), sem((2 * nz,)),
        ],
        compiler_params=pltpu.CompilerParams(collective_id=0, has_side_effects=True, vmem_limit_bytes=56 << 20),
    )(kernel.reshape(2 * rows, cols), data[:, 0])
    out = jax.ShapeDtypeStruct((2, 1, cols, width), F32)

    def q_map(n):
        def index(i):
            me = lax.axis_index("rx") // 2
            return (0, 0, 0, lax.rem(i * FIN + n - me + nz, nz), 0, 0)

        return index

    out_spec = pl.BlockSpec((2, 1, FIN * CH, width), lambda i: (0, 0, i, 0))
    return pl.pallas_call(
        functools.partial(finish_kernel, dims),
        name="finish",
        grid=(nz // FIN,),
        out_shape=(out, out),
        in_specs=[pl.BlockSpec((PH, G, 2, 1, R, CH), q_map(n)) for n in range(FIN)]
        + [pl.BlockSpec((ITERS + PH, 8, 128), lambda i: (0, 0, 0))],
        out_specs=(out_spec, out_spec),
        scratch_shapes=[vm((FIN, 2, 2, width, CH), F32)],
        compiler_params=pltpu.CompilerParams(vmem_limit_bytes=60 << 20),
    )(*([q_all] * FIN), coefs)


def solution(mesh):
    nx, ny, nz = mesh.shape["freq"], mesh.shape["src"], mesh.shape["rx"] // 2
    return jax.shard_map(
        functools.partial(on_device, nx, ny, nz),
        mesh=mesh,
        in_specs=(P(None, "freq", "rx", "src"), P(None, "freq", "rx", None)),
        out_specs=(P(None, "freq", "src", None), P(None, "freq", "src", None)),
        check_vma=False,
    )
```

time: 990 us -> 118 us (0.12)
  blocking collectives: 484 us -> 0 us
  waiting for transfers between devices: 432 us -> 0 us
  Pallas kernels: 0 us -> 117 us
  other arithmetic: 23.2 us -> 0 us
  matrix products: 18.4 us -> 0 us
  between operations: 18.6 us -> 0.64 us
    psum x6 -> x0, blocking collectives: 484 us -> none  [the longest x3 383 us: data_norm(): total = lax.psum(local, ('freq', 'rx'))]
    psum x5 -> x0, waiting for transfers between devices: 432 us -> none  [the longest x3 333 us: adjoint(): return lax.psum(partial_sum, 'rx')]
    pallas_call x0 -> x2, Pallas kernels: none -> 117 us  [the longest x1 112 us: on_device(): pl.pallas_call(functools.partial(lsqr_kernel, dims), name='lsqr', out_sha...]
    dot_general x10 -> x0, matrix products: 18.4 us -> none  [the longest x3 7.43 us: adjoint_term(): lax.dot_general(real_part, piece, dims, preferred_element_type=jnp.float32)]
    reduce_sum x6 -> x0, other arithmetic: 12.7 us -> none  [the longest x3 8.36 us: model_norm(): local = jnp.sum(field * field)]
  transfers between devices with their start and end apart: 5 -> 0, of which waited for: 5 -> 0; matrix products, arithmetic and copies ran while one was open for 0% -> 0% of each run, Pallas kernels for 0% -> 0%
where the time goes in v2:
time: 118 us
  Pallas kernels  117 us (99%)
    pallas_call x1, Pallas kernels, on_device(): pl.pallas_call(functools.partial(lsqr_kernel, dims), name='lsqr', out_sha...  112 us
    pallas_call x1, Pallas kernels, on_device(): pl.pallas_call(functools.partial(finish_kernel, dims), name='finish', gri...  5.31 us

profile of v2, /device:TPU:1, one launch (start us, length us, event | category | flops | bytes accessed | tf_op | source)
XLA Modules:
  0.0 117.7 jit_solution(12878839537425267005)
XLA Ops:
  0.6 111.7 %lsqr.1 = (bf16[3,1,2,8,128,256]{5,4,3,2,1,0:T(8,128)(2,1)}, f32[5,8,128]{2,1,0:T(8,128)}) custom-call(bf16[1024,2048]{1,0:T(8,128)(2,1)} %bitcast.2, f32[2,512,128]{2,1,0:T(8,128)} %bitcast.3), custom_call_target="tpu_custom_call" | custom-call | tf_op jit(solution)/shard_map/lsqr/pallas_call | solution.py:455
  112.4 5.3 %finish.1 = (f32[2,1,2048,128]{3,2,1,0:T(8,128)}, f32[2,1,2048,128]{3,2,1,0:T(8,128)}) custom-call(bf16[3,1,2,8,128,256]{5,4,3,2,1,0:T(8,128)(2,1)} %get-tuple-element.4.refs_0_.refs_1_.refs_2_.refs_3_, bf16[3,1,2,8,128,256]{5,4,3,2,1,0:T(8,128)(2,1)} %get-tuple-element.4.refs_0_.refs_1_.refs_2_.refs_3_, ...), custom_call_target="tpu_custom_call" | custom-call | tf_op jit(solution)/shard_map/finish/pallas_call | solution.py:509

commit v3 on v2

--- a/solution.py
+++ b/solution.py
@@ -34,12 +34,12 @@
 
 
 FAR = (4, 3, 5, 2, 6, 1, 7, 0)
-BATCHES = ((0, 2), (2, 3), (3, 5), (5, 8))
+BATCHES = ((0, 1), (1, 2), (2, 3), (3, 5), (5, 8))
 HILO = (True, True, False)
 
 
-def lsqr_kernel(dims, g_hbm, data_hbm, q_out, coef_ref, g_v, data_ref, d_t, p_st, lhs, own, q_prev, acc, sib_s, sib_r, rs_s, rs_r,
-                ag, y_s, y_r, nsq, sq_b, sp1_b, sp2_b, zc_b, g_sem, out_sem, sib_ss, sib_rs, rs_ss, rs_rs, ag_ss, ag_rs,
+def lsqr_kernel(dims, g_hbm, data_hbm, x_out, w1_out, q2_out, coef_ref, g_v, data_ref, d_t, p_st, lhs, own, q_prev, acc, sib_s, sib_r, rs_s, rs_r,
+                ag, y_s, y_r, nsq, sq_b, sp1_b, sp2_b, zc_b, out_buf, out_st, g_sem, out_sem, sib_ss, sib_rs, rs_ss, rs_rs, ag_ss, ag_rs,
                 as_ss, as_rs, y_ss, y_rs, sq_ss, sq_rs, sp1_ss, sp1_rs, sp2_ss, sp2_rs, zc_ss, zc_rs):
     nx, ny, nz, rows, cols, width = dims
     half = width // 2
@@ -155,25 +155,28 @@
             hi = u.astype(BF16)
             parts = (hi, (u - hi.astype(F32)).astype(BF16)) if HILO[k] else (hi,)
             for i, part in enumerate(parts):
-                r0 = (2 * i + pos) * R
-                lhs[g, r0 : r0 + R, :rows] = part
-                lhs[g, r0 : r0 + vr, rows:] = part[vr:]
-                lhs[g, r0 + vr : r0 + R, rows:] = -part[:vr]
-
-    def a1(k, g, batch):
-        for t in range(*BATCHES[batch]):
-            if k == 0 and g == 0:
+                r0 = i * R
+                lhs[g, pos, r0 : r0 + R, :rows] = part
+                lhs[g, pos, r0 : r0 + vr, rows:] = part[vr:]
+                lhs[g, pos, r0 + vr : r0 + R, rows:] = -part[:vr]
+
+    def a1(k, g, batch, pos):
+        t0, t1 = BATCHES[batch]
+        for t in range(t0, t1):
+            if k == 0 and g == 0 and pos == 1:
                 g_copy(t).wait()
             if HILO[k]:
-                res = lax.dot_general(lhs[g], g_v[:, lanes[FAR[t]]], NN, preferred_element_type=F32)
-                both = res[: 2 * R] + res[2 * R :]
+                res = lax.dot_general(lhs[g, pos], g_v[:, lanes[FAR[t]]], NN, preferred_element_type=F32)
+                res = res[:R] + res[R:]
             else:
-                both = lax.dot_general(lhs[g, : 2 * R], g_v[:, lanes[FAR[t]]], NN, preferred_element_type=F32)
-            own[g, t] = both[:R]
-            sib_s[k, g, t] = both[R:]
-        t0, t1 = BATCHES[batch]
-        part = pl.ds(t0, t1 - t0)
-        rc(sib_s.at[k, g, part], sib_r.at[k, g, part], sib_ss.at[k, g, batch], sib_rs.at[k, g, batch], sib)
+                res = lax.dot_general(lhs[g, pos, :R], g_v[:, lanes[FAR[t]]], NN, preferred_element_type=F32)
+            if pos == 0:
+                own[g, t] = res
+            else:
+                sib_s[k, g, t] = res
+        if pos:
+            part = pl.ds(t0, t1 - t0)
+            rc(sib_s.at[k, g, part], sib_r.at[k, g, part], sib_ss.at[k, g, batch], sib_rs.at[k, g, batch], sib)
 
     def rs_send(k, g, slot, to, lo=0, n=R):
         part = pl.ds(lo, n)
@@ -215,17 +218,18 @@
         rs_s[k, g, nz - 2, hr:] = (s[hr:] + rs_r[k, g, 0, hr:].astype(F32)).astype(BF16)
         rs_send(k, g, nz - 2, nz - 2)
 
-    def ag_send(k, g, rel, to, lo=0, n=R, sem=None):
+    def ag_send(k, g, rel, to, half=None):
         there = (rel - to) % nz
-        sem = there if sem is None else sem
-        rc(ag.at[k, g, 0, rel, pl.ds(lo, n)], ag.at[k, g, 0, there, pl.ds(lo, n)], ag_ss.at[k, g, sem], ag_rs.at[k, g, sem], zps[to])
-
-    def z_wait(k, g, rel):
-        if rel == 4:
-            wait_recv(ag.at[k, g, 0, 4, pl.ds(0, hr)], ag_ss.at[k, g, 4], ag_rs.at[k, g, 4])
-            wait_recv(ag.at[k, g, 0, 4, pl.ds(hr, hr)], ag_ss.at[k, g, 0], ag_rs.at[k, g, 0])
-        else:
-            wait_recv(ag.at[k, g, 0, rel], ag_ss.at[k, g, rel], ag_rs.at[k, g, rel])
+        rows_ = pl.ds(0, R) if half is None else pl.ds(half * hr, hr)
+        sems = (k, g, half or 0, there)
+        rc(ag.at[k, g, 0, rel, rows_], ag.at[k, g, 0, there, rows_], ag_ss.at[sems], ag_rs.at[sems], zps[to])
+
+    def z_wait(k, g, rel, half=None):
+        if rel in (1, nz - 1):
+            wait_recv(ag.at[k, g, 0, rel], ag_ss.at[k, g, 0, rel], ag_rs.at[k, g, 0, rel])
+            return
+        for h in (0, 1) if half is None else (half,):
+            wait_recv(ag.at[k, g, 0, rel, pl.ds(h * hr, hr)], ag_ss.at[k, g, h, rel], ag_rs.at[k, g, h, rel])
 
     def to_sib(k, g, rel, n=1):
         part = pl.ds(rel, n)
@@ -245,17 +249,23 @@
             q = q - coef * q_prev[g]
         q_prev[g] = q
         ag[k, g, 0, 0] = q.astype(BF16)
-        for to in (2, nz - 2, 1, nz - 1):
+        for to, h in ((nz - 2, 0), (2, 1), (nz - 2, 1), (2, 0)):
+            ag_send(k, g, 0, to, h)
+        for to in (1, nz - 1):
             ag_send(k, g, 0, to)
         to_sib(k, g, 0)
 
     def a4a(k, g):
-        z_wait(k, g, 2)
-        ag_send(k, g, 2, nz - 1)
-        ag_send(k, g, 2, nz - 2, 0, hr, 4)
-        z_wait(k, g, nz - 2)
-        ag_send(k, g, nz - 2, 1)
-        ag_send(k, g, nz - 2, 2, hr, hr, 0)
+        z_wait(k, g, 2, 0)
+        ag_send(k, g, 2, nz - 2, 0)
+        ag_send(k, g, 2, nz - 1, 0)
+        z_wait(k, g, nz - 2, 1)
+        ag_send(k, g, nz - 2, 2, 1)
+        ag_send(k, g, nz - 2, 1, 1)
+        z_wait(k, g, 2, 1)
+        ag_send(k, g, 2, nz - 1, 1)
+        z_wait(k, g, nz - 2, 0)
+        ag_send(k, g, nz - 2, 1, 0)
         z_wait(k, g, 1)
         to_sib(k, g, 1, 2)
         z_wait(k, g, nz - 1)
@@ -266,26 +276,28 @@
             z_wait(k, g, rel)
             to_sib(k, g, rel)
 
-    def f1(k, g, rel):
-        v0 = ag[k, g, 0, rel]
-        v1 = ag[k, g, 1, rel]
-        v = jnp.concatenate([v0, v1], axis=0)
-        w = jnp.concatenate([-v0[vr:], v0[:vr], -v1[vr:], v1[:vr]], axis=0)
+    def f1(k, g, rel, poss=(0, 1)):
+        vs = [ag[k, g, pos, rel] for pos in poss]
+        v = jnp.concatenate(vs, axis=0)
+        w = jnp.concatenate([h for u in vs for h in (-u[vr:], u[:vr])], axis=0)
         res = lax.dot_general(v, g_v[:rows, lanes[rel]], NT, preferred_element_type=F32)
         res = res + lax.dot_general(w, g_v[rows:, lanes[rel]], NT, preferred_element_type=F32)
+        sl = slice(poss[0] * R, (poss[-1] + 1) * R)
         if rel == 0:
-            acc[g] = res
+            acc[g, sl] = res
         else:
-            acc[g] += res
+            acc[g, sl] += res
 
     def q_norms(k, g, rel):
         for pos in range(2):
             nsq[g, pos, chunks[rel]] = tile_of_squares(ag[k, g, pos, rel].astype(F32))
 
-    YP = [(pos, slice(pos * R + n * hr, pos * R + n * hr + hr), 2 * n + pos) for n in range(2) for pos in range(2)]
-
-    def y_send(k, g, step):
+    YP = [(pos, slice(pos * R + n * hr, pos * R + n * hr + hr), 2 * n + pos) for pos in range(2) for n in range(2)]
+
+    def y_send(k, g, step, poss=(0, 1)):
         for pos, sl, i in YP:
+            if pos not in poss:
+                continue
             if step:
                 wait_recv(y_r.at[k, g, 0, sl], y_ss.at[k, g, 0, i], y_rs.at[k, g, 0, i])
                 acc[g, sl] = acc[g, sl] + y_r[k, g, 0, sl].astype(F32)
@@ -300,8 +312,37 @@
             rs = slice(sl.start - pos * R, sl.stop - pos * R)
             p_st[g, pos, rs] = total * inv_alpha - coef * p_st[g, pos, rs]
 
-    def out_copy(k):
-        return pltpu.make_async_copy(ag.at[k], q_out.at[k], out_sem.at[k])
+    def out_copy(o, rel):
+        dst = (x_out, w1_out, q2_out)[o].at[:, pl.ds(pl.multiple_of(chunks[rel] * CH, CH), CH)]
+        return pltpu.make_async_copy(out_st.at[o, rel], dst, out_sem.at[o, rel])
+
+    def out_chunk(o, rel, weights):
+        for g in G:
+            for pos in range(2):
+                h = core if pos == 0 else 1 - core
+                base = pl.multiple_of(h * half + g * vr, vr)
+                if weights is None:
+                    val = ag[ITERS, g, pos, rel]
+                else:
+                    val = sum(c * ag[j, g, pos, rel].astype(F32) for j, c in enumerate(weights)).astype(BF16)
+                for c in range(2):
+                    out_buf[o, rel, c, pl.ds(base, vr), :] = val[c * vr : (c + 1) * vr]
+        for c in range(2):
+            out_st[o, rel, c] = out_buf[o, rel, c].T
+        out_copy(o, rel).start()
+
+    recur = []
+
+    def advance(beta, alpha=None):
+        phibar, rhobar = recur_state[0]
+        rho = jnp.sqrt(rhobar * rhobar + beta * beta)
+        cosine, sine = rhobar / rho, beta / rho
+        if alpha is None:
+            return cosine * phibar / rho
+        recur_state[0] = (sine * phibar, -cosine * alpha)
+        recur.append((cosine * phibar / rho, sine * alpha / rho))
+
+    recur_state = [None]
 
     data_copy.wait()
     for c in range(2):
@@ -323,17 +364,24 @@
                 f2(k - 1, g, inv_alpha, alphas[-1] / betas[-1])
             if k or g:
                 build(k, g)
-            a1(k, g, 0)
-            a1(k, g, 1)
+            for batch in (0, 1, 2):
+                a1(k, g, batch, 1)
+            for batch in (0, 1, 2):
+                a1(k, g, batch, 0)
             if g == GROUPS - 1:
                 sp1_send(k)
-            a2(k, g, 0)
-            a2(k, g, 1)
-            a1(k, g, 2)
-        for g in G:
-            a1(k, g, 3)
-            a2(k, g, 2)
+            for batch in (0, 1, 2):
+                a2(k, g, batch)
+        for g in G:
+            for pos in (1, 0):
+                for batch in (3, 4):
+                    a1(k, g, batch, pos)
             a2(k, g, 3)
+            a2(k, g, 4)
+        if last:
+            w_1 = (-recur[0][1] / alphas[0], 1.0 / alphas[1])
+            for rel in range(nz):
+                out_chunk(1, rel, w_1)
         sp1_wait_sp2_send(k)
         for g in G:
             a2b(k, g)
@@ -344,17 +392,27 @@
             a3(k, g, inv_beta, coef)
         if last:
             last_norm_send(k)
+            step_2 = advance(betas[-1])
+            x_w = ((recur[0][0] - step_2 * recur[0][1]) / alphas[0], step_2 / alphas[1])
+            for rel in range(nz):
+                out_chunk(0, rel, x_w)
             for g in G:
                 a4a(k, g)
             last_norm_mid(k)
             for g in G:
+                for rel, n in ((0, 1), (1, 2), (nz - 2, 2)):
+                    sib_wait(k, g, rel, n)
+            for rel in (0, 1, 2, nz - 2, nz - 1):
+                out_chunk(2, rel, None)
+            for g in G:
                 a4b(k, g)
             drain()
-            for g in G:
-                for rel, n in ((0, 1), (1, 2), (nz - 2, 2), (3, 1), (nz - 3, 1), (4, 1)):
-                    sib_wait(k, g, rel, n)
-            out_copy(k).start()
+            for rel in (3, nz - 3, 4):
+                for g in G:
+                    sib_wait(k, g, rel)
+                out_chunk(2, rel, None)
             alphas.append(last_norm_wait())
+            advance(betas[-1], alphas[-1])
             break
         for g in G:
             sib_wait(k, g, 0)
@@ -372,77 +430,42 @@
             for rel in (0, 1, 2, nz - 2, nz - 1):
                 q_norms(k, g, rel)
         for g in G:
-            a4b(k, g)
+            for rel in (3, nz - 3, 4):
+                z_wait(k, g, rel)
+                to_sib(k, g, rel)
+                f1(k, g, rel, (0,))
+            y_send(k, g, 0, (0,))
         for g in G:
             for rel in (3, nz - 3, 4):
                 sib_wait(k, g, rel)
-                f1(k, g, rel)
-            y_send(k, g, 0)
+                f1(k, g, rel, (1,))
+            y_send(k, g, 0, (1,))
         for g in G:
             for rel in (3, nz - 3, 4):
                 q_norms(k, g, rel)
         sq_send(k)
-        out_copy(k).start()
         for g in G:
             y_send(k, g, 1)
         drain()
         alphas.append(jnp.sqrt(total_of(sq_tile(k))))
         inv_alpha = 1.0 / alphas[-1]
+        if k == 0:
+            recur_state[0] = (betas[0], alphas[0])
+        else:
+            advance(betas[-1], alphas[-1])
 
     factor = math.sqrt(2.0 * nx * cols * ny * width)
-    phibar, rhobar = betas[0], alphas[0]
-    x_w = [None] * PH
-    w_w = [1.0 / alphas[0]] + [None] * ITERS
-    for it in range(ITERS):
-        beta, alpha = betas[it + 1], alphas[it + 1]
-        rho = jnp.sqrt(rhobar * rhobar + beta * beta)
-        cosine, sine = rhobar / rho, beta / rho
-        theta = sine * alpha
-        rhobar = -cosine * alpha
-        phi = cosine * phibar
-        phibar = sine * phibar
-        step, back = phi / rho, theta / rho
-        for j in range(it + 1):
-            x_w[j] = step * w_w[j] if x_w[j] is None else x_w[j] + step * w_w[j]
-            w_w[j] = -back * w_w[j]
-        w_w[it + 1] = 1.0 / alpha
-    for j in range(ITERS):
-        coef_ref[j] = jnp.broadcast_to(x_w[j], (8, 128))
-    for j in range(PH):
-        coef_ref[ITERS + j] = jnp.broadcast_to(w_w[j] * factor, (8, 128))
-
-    for k in range(PH):
-        out_copy(k).wait()
-
-
-FIN = 4
-
-
-def finish_kernel(dims, *refs):
-    nx, ny, nz, rows, cols, width = dims
-    q_refs, (coef_ref, x_ref, w_ref, buf) = refs[:FIN], refs[FIN:]
-    half = width // 2
-    vr = half // GROUPS
-    core = lax.rem(lax.axis_index("rx"), 2)
-    cf = [coef_ref[j, 0:1, 0:1] for j in range(ITERS + PH)]
-    for n, q_ref in enumerate(q_refs):
-        for g in range(GROUPS):
-            for pos in range(2):
-                h = core if pos == 0 else 1 - core
-                base = pl.multiple_of(h * half + g * vr, vr)
-                q = [q_ref[k, g, pos, 0].astype(F32) for k in range(PH)]
-                xv = cf[0] * q[0]
-                for j in range(1, ITERS):
-                    xv = xv + cf[j] * q[j]
-                wv = cf[ITERS] * q[0]
-                for j in range(1, PH):
-                    wv = wv + cf[ITERS + j] * q[j]
-                for c in range(2):
-                    buf[n, 0, c, pl.ds(base, vr), :] = xv[c * vr : (c + 1) * vr]
-                    buf[n, 1, c, pl.ds(base, vr), :] = wv[c * vr : (c + 1) * vr]
-        for c in range(2):
-            x_ref[c, 0, n * CH : (n + 1) * CH] = buf[n, 0, c].T
-            w_ref[c, 0, n * CH : (n + 1) * CH] = buf[n, 1, c].T
+    coef_ref[0] = jnp.broadcast_to(factor / alphas[-1], (8, 128))
+    coef_ref[1] = jnp.broadcast_to(-factor * recur[-1][1], (8, 128))
+    for o in range(3):
+        for rel in range(nz):
+            out_copy(o, rel).wait()
+
+
+def finish_kernel(x_ref, w1_ref, q2_ref, coef_ref, x_out, w_out):
+    for c in range(2):
+        x_out[c, 0] = x_ref[c].astype(F32)
+        w_out[c, 0] = q2_ref[c].astype(F32) * coef_ref[0, 0:1, 0:1] + w1_ref[c].astype(F32) * coef_ref[1, 0:1, 0:1]
 
 
 def on_device(nx, ny, nz, kernel, data):
@@ -452,21 +475,25 @@
     G = GROUPS
     sem = pltpu.SemaphoreType.DMA
     vm = pltpu.VMEM
-    q_all, coefs = pl.pallas_call(
+    part = jax.ShapeDtypeStruct((2, cols, width), BF16)
+    hbm = pl.BlockSpec(memory_space=pl.ANY)
+    x_2, w_1, q_2, coefs = pl.pallas_call(
         functools.partial(lsqr_kernel, dims),
         name="lsqr",
         out_shape=(
-            jax.ShapeDtypeStruct((PH, G, 2, nz, R, CH), BF16),
-            jax.ShapeDtypeStruct((ITERS + PH, 8, 128), F32),
+            part,
+            part,
+            part,
+            jax.ShapeDtypeStruct((2, 8, 128), F32),
         ),
-        in_specs=[pl.BlockSpec(memory_space=pl.ANY), pl.BlockSpec(memory_space=pl.ANY)],
-        out_specs=(pl.BlockSpec(memory_space=pl.ANY), pl.BlockSpec(memory_space=pltpu.VMEM)),
+        in_specs=[hbm, hbm],
+        out_specs=(hbm, hbm, hbm, pl.BlockSpec(memory_space=pltpu.VMEM)),
         scratch_shapes=[
             vm((2 * rows, cols), BF16),
             vm((2, rows, width), F32),
             vm((2, width, rows), F32),
             vm((G, 2, R, rows), F32),
-            vm((G, 4 * R, 2 * rows), BF16),
+            vm((G, 2, 2 * R, 2 * rows), BF16),
             vm((G, nz, R, CH), F32),
             vm((G, R, CH), F32),
             vm((G, 2 * R, rows), F32),
@@ -482,11 +509,13 @@
             vm((PH, 2 * nx, 8, 128), F32),
             vm((PH, nz, 8, 128), F32),
             vm((2 * nz, 8, 128), F32),
+            vm((3, nz, 2, width, CH), BF16),
+            vm((3, nz, 2, CH, width), BF16),
             sem((nz + 1,)),
-            sem((PH,)),
+            sem((3, nz)),
             sem((PH, G, nz)), sem((PH, G, nz)),
             sem((PH, G, nz)), sem((PH, G, nz)),
-            sem((PH, G, nz)), sem((PH, G, nz)),
+            sem((PH, G, 2, nz)), sem((PH, G, 2, nz)),
             sem((PH, G, nz)), sem((PH, G, nz)),
             sem((ITERS, G, 2, 4)), sem((ITERS, G, 2, 4)),
             sem((PH, nx * ny)), sem((PH, nx * ny)),
@@ -497,26 +526,17 @@
         compiler_params=pltpu.CompilerParams(collective_id=0, has_side_effects=True, vmem_limit_bytes=56 << 20),
     )(kernel.reshape(2 * rows, cols), data[:, 0])
     out = jax.ShapeDtypeStruct((2, 1, cols, width), F32)
-
-    def q_map(n):
-        def index(i):
-            me = lax.axis_index("rx") // 2
-            return (0, 0, 0, lax.rem(i * FIN + n - me + nz, nz), 0, 0)
-
-        return index
-
-    out_spec = pl.BlockSpec((2, 1, FIN * CH, width), lambda i: (0, 0, i, 0))
+    blk = pl.BlockSpec((2, cols // 2, width), lambda i: (0, i, 0))
+    out_blk = pl.BlockSpec((2, 1, cols // 2, width), lambda i: (0, 0, i, 0))
     return pl.pallas_call(
-        functools.partial(finish_kernel, dims),
+        finish_kernel,
         name="finish",
-        grid=(nz // FIN,),
+        grid=(2,),
         out_shape=(out, out),
-        in_specs=[pl.BlockSpec((PH, G, 2, 1, R, CH), q_map(n)) for n in range(FIN)]
-        + [pl.BlockSpec((ITERS + PH, 8, 128), lambda i: (0, 0, 0))],
-        out_specs=(out_spec, out_spec),
-        scratch_shapes=[vm((FIN, 2, 2, width, CH), F32)],
+        in_specs=[blk, blk, blk, pl.BlockSpec((2, 8, 128), lambda i: (0, 0, 0))],
+        out_specs=(out_blk, out_blk),
         compiler_params=pltpu.CompilerParams(vmem_limit_bytes=60 << 20),
-    )(*([q_all] * FIN), coefs)
+    )(x_2, w_1, q_2, coefs)
 
 
 def solution(mesh):

time: 118 us -> 111 us (0.941)
  Pallas kernels: 117 us -> 110 us
    pallas_call x1, Pallas kernels: 112 us -> 106 us  [on_device(): pl.pallas_call(functools.partial(lsqr_kernel, dims), name='lsqr', out_sha...]
    pallas_call x1, Pallas kernels: 5.31 us -> 3.82 us  [on_device(): pl.pallas_call(finish_kernel, name='finish', grid=(2,), out_shape=(out, o...]
where the time goes in v3:
time: 111 us
  Pallas kernels  110 us (99%)
    pallas_call x1, Pallas kernels, on_device(): pl.pallas_call(functools.partial(lsqr_kernel, dims), name='lsqr', out_sha...  106 us
    pallas_call x1, Pallas kernels, on_device(): pl.pallas_call(finish_kernel, name='finish', grid=(2,), out_shape=(out, o...  3.82 us

profile of v3, /device:TPU:1, one launch (start us, length us, event | category | flops | bytes accessed | tf_op | source)
XLA Modules:
  0.0 110.8 jit_solution(4967781292428953264)
XLA Ops:
  0.6 106.3 %lsqr.1 = (bf16[2,2048,128]{2,1,0:T(8,128)(2,1)}, bf16[2,2048,128]{2,1,0:T(8,128)(2,1)}, bf16[2,2048,128]{2,1,0:T(8,128)(2,1)}, f32[2,8,128]{2,1,0:T(8,128)}) custom-call(bf16[1024,2048]{1,0:T(8,128)(2,1)} %bitcast.2, f32[2,512,128]{2,1,0:T(8,128)} %bitcast.3), custom_call_target="tpu_custom_call" | custom-call | tf_op jit(solution)/shard_map/lsqr/pallas_call | solution.py:480
  106.9 3.8 %finish.1 = (f32[2,1,2048,128]{3,2,1,0:T(8,128)}, f32[2,1,2048,128]{3,2,1,0:T(8,128)}) custom-call(bf16[2,2048,128]{2,1,0:T(8,128)(2,1)} %get-tuple-element.6.x_ref, bf16[2,2048,128]{2,1,0:T(8,128)(2,1)} %get-tuple-element.7.w1_ref, bf16[2,2048,128]{2,1,0:T(8,128)(2,1)} %get-tuple-element.8.q2_ref, f32[2,8,128]{2,1,0:T(8,128)} %get-tuple-element.9.coef_ref), custom_call_target="tpu_custom_call" | custom-call | tf_op jit(solution)/shard_map/finish/pallas_call | solution.py:531

commit v4 on v3

--- a/solution.py
+++ b/solution.py
@@ -39,8 +39,9 @@
 
 
 def lsqr_kernel(dims, g_hbm, data_hbm, x_out, w1_out, q2_out, coef_ref, g_v, data_ref, d_t, p_st, lhs, own, q_prev, acc, sib_s, sib_r, rs_s, rs_r,
-                ag, y_s, y_r, nsq, sq_b, sp1_b, sp2_b, zc_b, out_buf, out_st, g_sem, out_sem, sib_ss, sib_rs, rs_ss, rs_rs, ag_ss, ag_rs,
-                as_ss, as_rs, y_ss, y_rs, sq_ss, sq_rs, sp1_ss, sp1_rs, sp2_ss, sp2_rs, zc_ss, zc_rs):
+                ag, y_s, y_r, nsq, sq_b, sp1_b, sp2_b, zc_b, out_buf, out_st, g_sem, out_sem, send_sem, tile_rs, sib_rs, rs_rs,
+                ag_rs, as_rs, y_rs):
+    SIB, RS, AG, AS, Y, SQ, SP1, SP2, ZC = [send_sem.at[n] for n in range(9)]
     nx, ny, nz, rows, cols, width = dims
     half = width // 2
     vr = half // GROUPS
@@ -63,20 +64,28 @@
     chunks = [lax.rem(me + o, nz) for o in range(nz)]
     lanes = [pl.ds(pl.multiple_of(c * CH, CH), CH) for c in chunks]
 
-    started = []
-
     def rc(src, dst, ss, rs, dev):
-        c = pltpu.make_async_remote_copy(src_ref=src, dst_ref=dst, send_sem=ss, recv_sem=rs, device_id=dev, device_id_type=MESH)
-        c.start()
-        started.append(c)
-
-    def drain():
-        for c in started:
-            c.wait_send()
-        started.clear()
-
-    def wait_recv(dst, ss, rs):
-        pltpu.make_async_remote_copy(src_ref=dst, dst_ref=dst, send_sem=ss, recv_sem=rs, device_id=sib, device_id_type=MESH).wait_recv()
+        pltpu.make_async_remote_copy(src_ref=src, dst_ref=dst, send_sem=ss, recv_sem=rs, device_id=dev, device_id_type=MESH).start()
+
+    def wait_recv(dst, rs):
+        pltpu.make_async_remote_copy(src_ref=dst, dst_ref=dst, send_sem=SIB, recv_sem=rs, device_id=sib, device_id_type=MESH).wait_recv()
+
+    def wait_sent(src, ss):
+        pltpu.make_async_remote_copy(src_ref=src, dst_ref=src, send_sem=ss, recv_sem=tile_rs.at[0], device_id=sib, device_id_type=MESH).wait_send()
+
+    def drain(k):
+        for g in G:
+            wait_sent(sib_s.at[k, g], SIB)
+            wait_sent(rs_s.at[k, g, pl.ds(1, nz - 1)], RS)
+            wait_sent(ag.at[k, g, 0, pl.ds(1, nz - 1)], AG)
+            wait_sent(ag.at[k, g, 0], AS)
+            if k < ITERS:
+                wait_sent(y_s.at[k, g], Y)
+        wait_sent(sq_b.at[k, pl.ds(1, nx * ny - 1)], SQ)
+        wait_sent(sp1_b.at[k, pl.ds(1, 2 * nx - 1)], SP1)
+        wait_sent(sp2_b.at[k, pl.ds(1, nz - 1)], SP2)
+        if k == ITERS:
+            wait_sent(zc_b.at[pl.ds(1, 2 * nz - 1)], ZC)
 
     def g_copy(t):
         sl = lanes[FAR[t]]
@@ -93,12 +102,11 @@
 
     def tiles_send(buf, slot, tile, ss, rs, devs):
         buf[slot] = tile
-        for i, dev in enumerate(devs):
-            rc(buf.at[slot], buf.at[slot], ss.at[i], rs.at[slot], dev)
-
-    def tiles_wait(buf, n, slots, ss, rs):
-        for slot in slots:
-            wait_recv(buf.at[slot], ss.at[0], rs.at[slot])
+        for dev in devs:
+            rc(buf.at[slot], buf.at[slot], ss, rs, dev)
+
+    def tiles_wait(buf, n, rs):
+        wait_recv(buf.at[pl.ds(1, n - 1)], rs)
         tile = buf[0]
         for i in range(1, n):
             tile = tile + buf[i]
@@ -110,15 +118,14 @@
             for pos in range(2):
                 t = tile_of_squares(p_st[g, pos])
                 tile = t if tile is None else tile + t
-        tiles_send(sp1_b.at[k], 2 * x + core, tile, sp1_ss.at[k], sp1_rs.at[k], [sib] + xps[1:] + xcs[1:])
+        tiles_send(sp1_b.at[k], 2 * x + core, tile, SP1, tile_rs.at[PH + k], [sib] + xps[1:] + xcs[1:])
 
     def sp1_wait_sp2_send(k):
-        slots = [2 * lax.rem(x + dx, nx) + lax.rem(core + dc, 2) for dx in range(nx) for dc in range(2) if dx or dc]
-        tile = tiles_wait(sp1_b.at[k], 2 * nx, slots, sp1_ss.at[k], sp1_rs.at[k])
-        tiles_send(sp2_b.at[k], me, tile, sp2_ss.at[k], sp2_rs.at[k], zps[1:])
+        tile = tiles_wait(sp1_b.at[k], 2 * nx, tile_rs.at[PH + k])
+        tiles_send(sp2_b.at[k], me, tile, SP2, tile_rs.at[2 * PH + k], zps[1:])
 
     def sp2_wait(k):
-        return jnp.sqrt(total_of(tiles_wait(sp2_b.at[k], nz, chunks[1:], sp2_ss.at[k], sp2_rs.at[k])))
+        return jnp.sqrt(total_of(tiles_wait(sp2_b.at[k], nz, tile_rs.at[2 * PH + k])))
 
     def sq_send(k):
         total = None
@@ -129,25 +136,23 @@
                     part = part + nsq[g, pos, ch]
                 both = part if pos == 0 else both + part
             total = both if g == 0 else total + both
-        tiles_send(sq_b.at[k], x * ny + y, total, sq_ss.at[k], sq_rs.at[k], xys)
+        tiles_send(sq_b.at[k], x * ny + y, total, SQ, tile_rs.at[k], xys)
 
     def sq_tile(k):
-        slots = [lax.rem(x + dx, nx) * ny + lax.rem(y + dy, ny) for dx, dy in xy]
-        return tiles_wait(sq_b.at[k], nx * ny, slots, sq_ss.at[k], sq_rs.at[k])
+        return tiles_wait(sq_b.at[k], nx * ny, tile_rs.at[k])
 
     def last_norm_send(k):
         total = None
         for g in G:
             t = tile_of_squares(ag[k, g, 0, 0].astype(F32))
             total = t if total is None else total + t
-        tiles_send(sq_b.at[k], x * ny + y, total, sq_ss.at[k], sq_rs.at[k], xys)
+        tiles_send(sq_b.at[k], x * ny + y, total, SQ, tile_rs.at[k], xys)
 
     def last_norm_mid(k):
-        tiles_send(zc_b, rx, sq_tile(k), zc_ss, zc_rs, zcs + zps[1:])
+        tiles_send(zc_b, rx, sq_tile(k), ZC, tile_rs.at[3 * PH], zcs + zps[1:])
 
     def last_norm_wait():
-        slots = [lax.rem(rx + d, 2 * nz) for d in range(1, 2 * nz)]
-        return jnp.sqrt(total_of(tiles_wait(zc_b, 2 * nz, slots, zc_ss, zc_rs)))
+        return jnp.sqrt(total_of(tiles_wait(zc_b, 2 * nz, tile_rs.at[3 * PH])))
 
     def build(k, g):
         for pos in range(2):
@@ -174,22 +179,24 @@
                 own[g, t] = res
             else:
                 sib_s[k, g, t] = res
-        if pos:
-            part = pl.ds(t0, t1 - t0)
-            rc(sib_s.at[k, g, part], sib_r.at[k, g, part], sib_ss.at[k, g, batch], sib_rs.at[k, g, batch], sib)
+
+    def sib_send(k, g, batch):
+        t0, t1 = BATCHES[batch]
+        part = pl.ds(t0, t1 - t0)
+        rc(sib_s.at[k, g, part], sib_r.at[k, g, part], SIB, sib_rs.at[k, g, batch], sib)
 
     def rs_send(k, g, slot, to, lo=0, n=R):
         part = pl.ds(lo, n)
-        rc(rs_s.at[k, g, slot, part], rs_r.at[k, g, slot, part], rs_ss.at[k, g, slot], rs_rs.at[k, g, slot], zps[to])
+        rc(rs_s.at[k, g, slot, part], rs_r.at[k, g, slot, part], RS, rs_rs.at[k, g, slot], zps[to])
 
     def rs_wait(k, g, slot, lo=0, n=R):
         part = pl.ds(lo, n)
-        wait_recv(rs_r.at[k, g, slot, part], rs_ss.at[k, g, slot], rs_rs.at[k, g, slot])
+        wait_recv(rs_r.at[k, g, slot, part], rs_rs.at[k, g, slot])
 
     def a2(k, g, batch):
         t0, t1 = BATCHES[batch]
         part = pl.ds(t0, t1 - t0)
-        wait_recv(sib_r.at[k, g, part], sib_ss.at[k, g, batch], sib_rs.at[k, g, batch])
+        wait_recv(sib_r.at[k, g, part], sib_rs.at[k, g, batch])
         for t in range(t0, t1):
             off = FAR[t]
             pair = own[g, t] + sib_r[k, g, t]
@@ -218,26 +225,25 @@
         rs_s[k, g, nz - 2, hr:] = (s[hr:] + rs_r[k, g, 0, hr:].astype(F32)).astype(BF16)
         rs_send(k, g, nz - 2, nz - 2)
 
+    def ag_sem(k, g, rel, half):
+        return ag_rs.at[k, g, {(2, 1): 0, (nz - 2, 0): nz}.get((rel, half), rel)]
+
     def ag_send(k, g, rel, to, half=None):
         there = (rel - to) % nz
-        rows_ = pl.ds(0, R) if half is None else pl.ds(half * hr, hr)
-        sems = (k, g, half or 0, there)
-        rc(ag.at[k, g, 0, rel, rows_], ag.at[k, g, 0, there, rows_], ag_ss.at[sems], ag_rs.at[sems], zps[to])
+        part = pl.ds(0, R) if half is None else pl.ds(half * hr, hr)
+        rc(ag.at[k, g, 0, rel, part], ag.at[k, g, 0, there, part], AG, ag_sem(k, g, there, half), zps[to])
 
     def z_wait(k, g, rel, half=None):
-        if rel in (1, nz - 1):
-            wait_recv(ag.at[k, g, 0, rel], ag_ss.at[k, g, 0, rel], ag_rs.at[k, g, 0, rel])
-            return
-        for h in (0, 1) if half is None else (half,):
-            wait_recv(ag.at[k, g, 0, rel, pl.ds(h * hr, hr)], ag_ss.at[k, g, h, rel], ag_rs.at[k, g, h, rel])
+        part = pl.ds(0, R) if half is None else pl.ds(half * hr, hr)
+        wait_recv(ag.at[k, g, 0, rel, part], ag_sem(k, g, rel, half))
 
     def to_sib(k, g, rel, n=1):
         part = pl.ds(rel, n)
-        rc(ag.at[k, g, 0, part], ag.at[k, g, 1, part], as_ss.at[k, g, rel], as_rs.at[k, g, rel], sib)
+        rc(ag.at[k, g, 0, part], ag.at[k, g, 1, part], AS, as_rs.at[k, g, rel], sib)
 
     def sib_wait(k, g, rel, n=1):
         part = pl.ds(rel, n)
-        wait_recv(ag.at[k, g, 1, part], as_ss.at[k, g, rel], as_rs.at[k, g, rel])
+        wait_recv(ag.at[k, g, 1, part], as_rs.at[k, g, rel])
 
     def a3(k, g, inv_beta, coef):
         s = own[g, FAR.index(0)]
@@ -299,22 +305,22 @@
             if pos not in poss:
                 continue
             if step:
-                wait_recv(y_r.at[k, g, 0, sl], y_ss.at[k, g, 0, i], y_rs.at[k, g, 0, i])
+                wait_recv(y_r.at[k, g, 0, sl], y_rs.at[k, g, 0, i])
                 acc[g, sl] = acc[g, sl] + y_r[k, g, 0, sl].astype(F32)
             y_s[k, g, step, sl] = acc[g, sl].astype(BF16)
             dev = ynb[(pos + step) % 2]
-            rc(y_s.at[k, g, step, sl], y_r.at[k, g, step, sl], y_ss.at[k, g, step, i], y_rs.at[k, g, step, i], dev)
+            rc(y_s.at[k, g, step, sl], y_r.at[k, g, step, sl], Y, y_rs.at[k, g, step, i], dev)
 
     def f2(k, g, inv_alpha, coef):
         for pos, sl, i in YP:
-            wait_recv(y_r.at[k, g, 1, sl], y_ss.at[k, g, 1, i], y_rs.at[k, g, 1, i])
+            wait_recv(y_r.at[k, g, 1, sl], y_rs.at[k, g, 1, i])
             total = acc[g, sl] + y_r[k, g, 1, sl].astype(F32)
             rs = slice(sl.start - pos * R, sl.stop - pos * R)
             p_st[g, pos, rs] = total * inv_alpha - coef * p_st[g, pos, rs]
 
     def out_copy(o, rel):
         dst = (x_out, w1_out, q2_out)[o].at[:, pl.ds(pl.multiple_of(chunks[rel] * CH, CH), CH)]
-        return pltpu.make_async_copy(out_st.at[o, rel], dst, out_sem.at[o, rel])
+        return pltpu.make_async_copy(out_st.at[o, rel], dst, out_sem.at[o])
 
     def out_chunk(o, rel, weights):
         for g in G:
@@ -354,7 +360,6 @@
             for c in range(2):
                 p_st[g, pos, c * vr : (c + 1) * vr, :] = d_t[c, pl.ds(base, vr), :]
     build(0, 0)
-    pl.semaphore_wait(barrier, len(peers))
 
     alphas, betas = [], []
     for k in range(PH):
@@ -364,18 +369,31 @@
                 f2(k - 1, g, inv_alpha, alphas[-1] / betas[-1])
             if k or g:
                 build(k, g)
-            for batch in (0, 1, 2):
-                a1(k, g, batch, 1)
-            for batch in (0, 1, 2):
-                a1(k, g, batch, 0)
+            if k == 0:
+                for pos in (1, 0):
+                    for batch in range(5):
+                        a1(k, g, batch, pos)
+                if g == 0:
+                    pl.semaphore_wait(barrier, len(peers))
+                for batch in range(5):
+                    sib_send(k, g, batch)
+            else:
+                for batch in (0, 1, 2):
+                    a1(k, g, batch, 1)
+                    sib_send(k, g, batch)
+                for batch in (0, 1, 2):
+                    a1(k, g, batch, 0)
             if g == GROUPS - 1:
                 sp1_send(k)
             for batch in (0, 1, 2):
                 a2(k, g, batch)
         for g in G:
-            for pos in (1, 0):
+            if k:
                 for batch in (3, 4):
-                    a1(k, g, batch, pos)
+                    a1(k, g, batch, 1)
+                    sib_send(k, g, batch)
+                for batch in (3, 4):
+                    a1(k, g, batch, 0)
             a2(k, g, 3)
             a2(k, g, 4)
         if last:
@@ -406,12 +424,12 @@
                 out_chunk(2, rel, None)
             for g in G:
                 a4b(k, g)
-            drain()
             for rel in (3, nz - 3, 4):
                 for g in G:
                     sib_wait(k, g, rel)
                 out_chunk(2, rel, None)
             alphas.append(last_norm_wait())
+            drain(k)
             advance(betas[-1], alphas[-1])
             break
         for g in G:
@@ -446,7 +464,7 @@
         sq_send(k)
         for g in G:
             y_send(k, g, 1)
-        drain()
+        drain(k)
         alphas.append(jnp.sqrt(total_of(sq_tile(k))))
         inv_alpha = 1.0 / alphas[-1]
         if k == 0:
@@ -458,8 +476,7 @@
     coef_ref[0] = jnp.broadcast_to(factor / alphas[-1], (8, 128))
     coef_ref[1] = jnp.broadcast_to(-factor * recur[-1][1], (8, 128))
     for o in range(3):
-        for rel in range(nz):
-            out_copy(o, rel).wait()
+        pltpu.make_async_copy(out_st.at[o], out_st.at[o], out_sem.at[o]).wait()
 
 
 def finish_kernel(x_ref, w1_ref, q2_ref, coef_ref, x_out, w_out):
@@ -512,16 +529,14 @@
             vm((3, nz, 2, width, CH), BF16),
             vm((3, nz, 2, CH, width), BF16),
             sem((nz + 1,)),
-            sem((3, nz)),
-            sem((PH, G, nz)), sem((PH, G, nz)),
-            sem((PH, G, nz)), sem((PH, G, nz)),
-            sem((PH, G, 2, nz)), sem((PH, G, 2, nz)),
-            sem((PH, G, nz)), sem((PH, G, nz)),
-            sem((ITERS, G, 2, 4)), sem((ITERS, G, 2, 4)),
-            sem((PH, nx * ny)), sem((PH, nx * ny)),
-            sem((PH, 2 * nx)), sem((PH, 2 * nx)),
-            sem((PH, nz)), sem((PH, nz)),
-            sem((2 * nz,)), sem((2 * nz,)),
+            sem((3,)),
+            sem((9,)),
+            sem((3 * PH + 1,)),
+            sem((PH, G, 5)),
+            sem((PH, G, nz)),
+            sem((PH, G, nz + 1)),
+            sem((PH, G, nz)),
+            sem((ITERS, G, 2, 4)),
         ],
         compiler_params=pltpu.CompilerParams(collective_id=0, has_side_effects=True, vmem_limit_bytes=56 << 20),
     )(kernel.reshape(2 * rows, cols), data[:, 0])

time: 111 us -> 108 us (0.973)
  Pallas kernels: 110 us -> 107 us
    pallas_call x1, Pallas kernels: 106 us -> 103 us  [on_device(): pl.pallas_call(functools.partial(lsqr_kernel, dims), name='lsqr', out_sha...]
where the time goes in v4:
time: 108 us; the launch traced here: 107 us
  Pallas kernels  107 us (99%)
    pallas_call x1, Pallas kernels, on_device(): pl.pallas_call(functools.partial(lsqr_kernel, dims), name='lsqr', out_sha...  103 us
    pallas_call x1, Pallas kernels, on_device(): pl.pallas_call(finish_kernel, name='finish', grid=(2,), out_shape=(out, o...  3.82 us

profile of v4, /device:TPU:1, one launch (start us, length us, event | category | flops | bytes accessed | tf_op | source)
XLA Modules:
  0.0 107.4 jit_solution(8855970351988586534)
XLA Ops:
  0.6 103.0 %lsqr.1 = (bf16[2,2048,128]{2,1,0:T(8,128)(2,1)}, bf16[2,2048,128]{2,1,0:T(8,128)(2,1)}, bf16[2,2048,128]{2,1,0:T(8,128)(2,1)}, f32[2,8,128]{2,1,0:T(8,128)}) custom-call(bf16[1024,2048]{1,0:T(8,128)(2,1)} %bitcast.2, f32[2,512,128]{2,1,0:T(8,128)} %bitcast.3), custom_call_target="tpu_custom_call" | custom-call | tf_op jit(solution)/shard_map/lsqr/pallas_call | solution.py:497
  103.6 3.8 %finish.1 = (f32[2,1,2048,128]{3,2,1,0:T(8,128)}, f32[2,1,2048,128]{3,2,1,0:T(8,128)}) custom-call(bf16[2,2048,128]{2,1,0:T(8,128)(2,1)} %get-tuple-element.6.x_ref, bf16[2,2048,128]{2,1,0:T(8,128)(2,1)} %get-tuple-element.7.w1_ref, bf16[2,2048,128]{2,1,0:T(8,128)(2,1)} %get-tuple-element.8.q2_ref, f32[2,8,128]{2,1,0:T(8,128)} %get-tuple-element.9.coef_ref), custom_call_target="tpu_custom_call" | custom-call | tf_op jit(solution)/shard_map/finish/pallas_call | solution.py:546

commit v5 on v4

--- a/solution.py
+++ b/solution.py
@@ -185,13 +185,13 @@
         part = pl.ds(t0, t1 - t0)
         rc(sib_s.at[k, g, part], sib_r.at[k, g, part], SIB, sib_rs.at[k, g, batch], sib)
 
-    def rs_send(k, g, slot, to, lo=0, n=R):
-        part = pl.ds(lo, n)
-        rc(rs_s.at[k, g, slot, part], rs_r.at[k, g, slot, part], RS, rs_rs.at[k, g, slot], zps[to])
-
-    def rs_wait(k, g, slot, lo=0, n=R):
-        part = pl.ds(lo, n)
-        wait_recv(rs_r.at[k, g, slot, part], rs_rs.at[k, g, slot])
+    def rs_send(k, g, slot, to, half=None):
+        part = pl.ds(0, R) if half is None else pl.ds(half * hr, hr)
+        rc(rs_s.at[k, g, slot, part], rs_r.at[k, g, slot, part], RS, rs_rs.at[k, g, half or 0, slot], zps[to])
+
+    def rs_wait(k, g, slot, half=None):
+        part = pl.ds(0, R) if half is None else pl.ds(half * hr, hr)
+        wait_recv(rs_r.at[k, g, slot, part], rs_rs.at[k, g, half or 0, slot])
 
     def a2(k, g, batch):
         t0, t1 = BATCHES[batch]
@@ -200,30 +200,34 @@
         for t in range(t0, t1):
             off = FAR[t]
             pair = own[g, t] + sib_r[k, g, t]
+            if off in (0, 2, nz - 2):
+                own[g, t] = pair
+                continue
+            rs_s[k, g, off] = pair.astype(BF16)
             if off == 4:
-                rs_s[k, g, 4, :hr] = pair[:hr].astype(BF16)
-                rs_s[k, g, 0, hr:] = pair[hr:].astype(BF16)
-                rs_send(k, g, 4, 2, 0, hr)
-                rs_send(k, g, 0, nz - 2, hr, hr)
-            elif off in (0, 2, nz - 2):
-                own[g, t] = pair
+                rs_send(k, g, 4, 2, 0)
+                rs_send(k, g, 4, nz - 2, 1)
+            elif off == 3:
+                rs_send(k, g, 3, 1, 1)
+                rs_send(k, g, 3, 1, 0)
+            elif off == nz - 3:
+                rs_send(k, g, off, nz - 1, 0)
+                rs_send(k, g, off, nz - 1, 1)
             else:
-                rs_s[k, g, off] = pair.astype(BF16)
-                rs_send(k, g, off, 1 if off in (1, 3) else nz - 1)
+                rs_send(k, g, off, off)
 
     def a2b(k, g):
-        rs_wait(k, g, 3)
-        rs_wait(k, g, 4, 0, hr)
-        s = own[g, FAR.index(2)] + rs_r[k, g, 3].astype(F32)
-        rs_s[k, g, 2, :hr] = (s[:hr] + rs_r[k, g, 4, :hr].astype(F32)).astype(BF16)
-        rs_s[k, g, 2, hr:] = s[hr:].astype(BF16)
-        rs_send(k, g, 2, 2)
-        rs_wait(k, g, nz - 3)
-        rs_wait(k, g, 0, hr, hr)
-        s = own[g, FAR.index(nz - 2)] + rs_r[k, g, nz - 3].astype(F32)
-        rs_s[k, g, nz - 2, :hr] = s[:hr].astype(BF16)
-        rs_s[k, g, nz - 2, hr:] = (s[hr:] + rs_r[k, g, 0, hr:].astype(F32)).astype(BF16)
-        rs_send(k, g, nz - 2, nz - 2)
+        for h in (1, 0):
+            for off, near, first in ((2, 3, 1), (nz - 2, nz - 3, 0)):
+                part = first if h else 1 - first
+                sl = slice(part * hr, part * hr + hr)
+                rs_wait(k, g, near, part)
+                s = own[g, FAR.index(off), sl] + rs_r[k, g, near, sl].astype(F32)
+                if not h:
+                    rs_wait(k, g, 4, part)
+                    s = s + rs_r[k, g, 4, sl].astype(F32)
+                rs_s[k, g, off, sl] = s.astype(BF16)
+                rs_send(k, g, off, off, part)
 
     def ag_sem(k, g, rel, half):
         return ag_rs.at[k, g, {(2, 1): 0, (nz - 2, 0): nz}.get((rel, half), rel)]
@@ -247,8 +251,12 @@
 
     def a3(k, g, inv_beta, coef):
         s = own[g, FAR.index(0)]
-        for off in (1, nz - 1, 2, nz - 2):
+        for off in (1, nz - 1):
             rs_wait(k, g, off)
+            s = s + rs_r[k, g, off].astype(F32)
+        for off in (2, nz - 2):
+            rs_wait(k, g, off, 0)
+            rs_wait(k, g, off, 1)
             s = s + rs_r[k, g, off].astype(F32)
         q = s * inv_beta
         if k:
@@ -533,7 +541,7 @@
             sem((9,)),
             sem((3 * PH + 1,)),
             sem((PH, G, 5)),
-            sem((PH, G, nz)),
+            sem((PH, G, 2, nz)),
             sem((PH, G, nz + 1)),
             sem((PH, G, nz)),
             sem((ITERS, G, 2, 4)),

time: 108 us -> 107 us (level)
  no operation moved by 1% of the time
where the time goes in v5:
time: 107 us
  Pallas kernels  107 us (100%)
    pallas_call x1, Pallas kernels, on_device(): pl.pallas_call(functools.partial(lsqr_kernel, dims), name='lsqr', out_sha...  103 us
    pallas_call x1, Pallas kernels, on_device(): pl.pallas_call(finish_kernel, name='finish', grid=(2,), out_shape=(out, o...  3.82 us

profile of v5, /device:TPU:1, one launch (start us, length us, event | category | flops | bytes accessed | tf_op | source)
XLA Modules:
  0.0 107.2 jit_solution(6949054365287044137)
XLA Ops:
  0.6 102.7 %lsqr.1 = (bf16[2,2048,128]{2,1,0:T(8,128)(2,1)}, bf16[2,2048,128]{2,1,0:T(8,128)(2,1)}, bf16[2,2048,128]{2,1,0:T(8,128)(2,1)}, f32[2,8,128]{2,1,0:T(8,128)}) custom-call(bf16[1024,2048]{1,0:T(8,128)(2,1)} %bitcast.2, f32[2,512,128]{2,1,0:T(8,128)} %bitcast.3), custom_call_target="tpu_custom_call" | custom-call | tf_op jit(solution)/shard_map/lsqr/pallas_call | solution.py:505
  103.4 3.8 %finish.1 = (f32[2,1,2048,128]{3,2,1,0:T(8,128)}, f32[2,1,2048,128]{3,2,1,0:T(8,128)}) custom-call(bf16[2,2048,128]{2,1,0:T(8,128)(2,1)} %get-tuple-element.6.x_ref, bf16[2,2048,128]{2,1,0:T(8,128)(2,1)} %get-tuple-element.7.w1_ref, bf16[2,2048,128]{2,1,0:T(8,128)(2,1)} %get-tuple-element.8.q2_ref, f32[2,8,128]{2,1,0:T(8,128)} %get-tuple-element.9.coef_ref), custom_call_target="tpu_custom_call" | custom-call | tf_op jit(solution)/shard_map/finish/pallas_call | solution.py:554
